TPU v7x, 32 devices: a whole 2x2x4 slice. The times are simulated.
32 devices in a mesh: seq: 4 (over x, core), fsdp: 8 (over z, y).
Axes of the slice: x: 2, y: 2, z: 4, core: 2. Of those that a mesh axis runs over, the one named last changes fastest.
Arguments:
- tokens: bfloat16 [65536, 512], P(('fsdp', 'seq')), may hold values from -6 to 6
- doc_ids: int32 [8, 8192], P('fsdp', 'seq'), may hold values from 0 to 31, never falling along the last dimension, each value on 1 to 4096 neighbouring positions
- w_query: float32 [512, 512], P('fsdp'), may hold values from -0.375 to 0.375
- w_key: float32 [512, 512], P('fsdp'), may hold values from -0.375 to 0.375
- w_value: float32 [512, 512], P('fsdp'), may hold values from -0.25 to 0.25
- w_slots: float32 [512, 512], P('fsdp'), may hold values from -0.5 to 0.5
- w_output: float32 [512, 512], P('fsdp'), may hold values from -0.75 to 0.75
- w_hidden: float32 [512, 2048], P('fsdp'), may hold values from -0.25 to 0.25
- w_return: float32 [2048, 512], P('fsdp'), may hold values from -0.1875 to 0.1875
- gain_first: float32 [512], P('fsdp'), may hold values from 0.1 to 1.9
- shift_first: float32 [512], P('fsdp'), may hold values from -3 to 3
- gain_second: float32 [512], P('fsdp'), may hold values from 0.1 to 1.9
- shift_second: float32 [512], P('fsdp'), may hold values from -3 to 3
- bias_hidden: float32 [2048], P('fsdp'), may hold values from -3 to 3
- bias_return: float32 [512], P('fsdp'), may hold values from -3 to 3
- cotangent: bfloat16 [65536, 512], P(('fsdp', 'seq')), may hold values from -6 to 6
Outputs:
- layer_out: bfloat16 [65536, 512], P(('fsdp', 'seq'))
- grad_input: float32 [65536, 512], P(('fsdp', 'seq'))
- grad_w_query: float32 [512, 512], P('fsdp')
- grad_w_key: float32 [512, 512], P('fsdp')
- grad_w_value: float32 [512, 512], P('fsdp')
- grad_w_slots: float32 [512, 512], P('fsdp')
- grad_w_output: float32 [512, 512], P('fsdp')
- grad_w_hidden: float32 [512, 2048], P('fsdp')
- grad_w_return: float32 [2048, 512], P('fsdp')
- grad_gain_first: float32 [512], P('fsdp')
- grad_shift_first: float32 [512], P('fsdp')
- grad_gain_second: float32 [512], P('fsdp')
- grad_shift_second: float32 [512], P('fsdp')
- grad_bias_hidden: float32 [2048], P('fsdp')
- grad_bias_return: float32 [512], P('fsdp')
Inputs may be any that keep to these rules, and one draw needn't show every extreme that they name: `doc_ids`: in each packed sequence the document numbers never fall, each document has at least one token, and at most 4096 tokens, with one document of exactly 4096 tokens.
All inputs are finite; a program needn't handle non-finite values.
Results may differ from a plain program's by a relative error of at most 0.01.
The roundings to bfloat16 on the way count: a program that leaves them out, or rounds other values in their place, can miss the bound.
Values may be sent and summed in bfloat16 or wider, within the bound.
A program may use at most 192 MiB of HBM per device.

v0:
```python
import functools
import types

import jax
import jax.numpy as jnp
from jax import lax
from jax.experimental import pallas as pl
from jax.experimental.pallas import tpu as pltpu
from jax.sharding import PartitionSpec as P

D = 512
H = 8
M = 64
FF = 2048
C = 256
GROUP = 256
EPS = 1e-05
SCALE = 0.125
F32 = jnp.float32
BF16 = jnp.bfloat16
FEED_ROWS = 512
FEED_LANES = 256
FRONT = 4
MIB = 1024 * 1024


def dot(a, b):
    return lax.dot_general(a, b, (((1,), (0,)), ((), ())), preferred_element_type=F32)


def dot_nt(a, b):
    return lax.dot_general(a, b, (((1,), (1,)), ((), ())), preferred_element_type=F32)


def dot_tn(a, b):
    return lax.dot_general(a, b, (((0,), (0,)), ((), ())), preferred_element_type=F32)


def lane_heads(rows, lanes):
    return lax.broadcasted_iota(jnp.int32, (rows, lanes), 1) // M


def stacked(values):
    heads = lane_heads(C, GROUP)
    zero = jnp.zeros_like(values)
    return jnp.concatenate([jnp.where(heads == h, values, zero) for h in range(4)], axis=0)


def select(values):
    heads = lane_heads(C, GROUP)
    out = values[3 * C :]
    for h in (2, 1, 0):
        out = jnp.where(heads == h, values[h * C : (h + 1) * C], out)
    return out


def masked(values, mask):
    return jnp.concatenate(
        [values[h * C : (h + 1) * C].astype(BF16) * mask for h in range(4)], axis=0
    )


def expand(compact):
    rows = lax.broadcasted_iota(jnp.int32, (GROUP, GROUP), 0) // M
    full = jnp.concatenate([compact] * 4, axis=0)
    return jnp.where(rows == lane_heads(GROUP, GROUP), full, jnp.zeros_like(full))


def compacted(full):
    heads = lane_heads(M, GROUP)
    out = full[3 * M :]
    for h in (2, 1, 0):
        out = jnp.where(heads == h, full[h * M : (h + 1) * M], out)
    return out


def split(values):
    high = values.astype(BF16)
    return high, (values - high.astype(F32)).astype(BF16)


def ones_block():
    rows = lax.broadcasted_iota(jnp.int32, (GROUP, GROUP), 0) // M
    return (rows == lane_heads(GROUP, GROUP)).astype(BF16)


def head_sums(values):
    high, low = split(values)
    ones = ones_block()
    return dot(high, ones) + dot(low, ones)


def head_max(values):
    left = lane_heads(C, 128) == 0
    out = []
    for p in range(2):
        pair = values[:, p * 128 : (p + 1) * 128]
        one = jnp.max(jnp.where(left, pair, -jnp.inf), axis=1, keepdims=True)
        two = jnp.max(jnp.where(left, -jnp.inf, pair), axis=1, keepdims=True)
        out.append(jnp.where(left, one, two))
    return jnp.concatenate(out, axis=1)


def wide(values, times):
    return jnp.concatenate([values] * times, axis=1)


def visible(doc_col, doc_row):
    same = wide(doc_col, 2) == doc_row
    here = lax.broadcasted_iota(jnp.int32, (C, C), 0)
    there = lax.broadcasted_iota(jnp.int32, (C, C), 1)
    return jnp.where(same & (here >= there), 1.0, 0.0).astype(BF16)


def visible_back(doc_col, doc_row):
    same = wide(doc_col, 2) == doc_row
    here = lax.broadcasted_iota(jnp.int32, (C, C), 0)
    there = lax.broadcasted_iota(jnp.int32, (C, C), 1)
    return jnp.where(same & (there >= here), 1.0, 0.0).astype(BF16)


def flag(doc_col, doc):
    return jnp.where(doc_col == doc[:, :128], 1.0, 0.0)


def norm_parts(values):
    centre = jnp.mean(values, axis=-1, keepdims=True)
    centred = values - centre
    spread = jnp.mean(centred * centred, axis=-1, keepdims=True)
    scale = lax.rsqrt(spread + EPS)
    return centred * scale, scale


def norm_back(unit, scale, gain, grad):
    inner = grad * gain
    return scale * (
        inner
        - jnp.mean(inner, axis=-1, keepdims=True)
        - unit * jnp.mean(inner * unit, axis=-1, keepdims=True)
    )


def groups(values):
    return values[:, :GROUP], values[:, GROUP:]


def state_terms(slots, left, right):
    one, two = [], []
    for g in range(2):
        lanes = slice(g * GROUP, (g + 1) * GROUP)
        both = dot_tn(slots[:, lanes], jnp.concatenate([left[:, lanes], right[:, lanes]], axis=1))
        one.append(compacted(both[:, :GROUP]))
        two.append(compacted(both[:, GROUP:]))
    return jnp.concatenate(one, axis=1), jnp.concatenate(two, axis=1)


def lanes_of(g):
    return slice(g * GROUP, (g + 1) * GROUP)


def part_of(ref, part, g):
    return ref[:, part * D + g * GROUP : part * D + (g + 1) * GROUP]


def attend_body(
    n, qkvf_ref, slots, vis, col, edge_ref, state, o_ref, p_ref, s_ref, z_ref, kept_ref
):
    kept_ref[0] = state[0:128]
    first = edge_ref[pl.ds(0, 1)]
    before = edge_ref[pl.ds(8 + jnp.maximum(n - 1, 0), 1)]
    last = jnp.where(n == 0, first, before)
    newest = edge_ref[pl.ds(8 + n, 1)]
    carried = wide(flag(col, last), 2)
    norm = dot(vis, slots)
    key_states = [expand(state[0:64, lanes_of(g)]).astype(BF16) for g in range(2)]
    value_states = [expand(state[64:128, lanes_of(g)]).astype(BF16) for g in range(2)]
    norm_state = state[128:129]

    def affine(g):
        return masked(dot_nt(stacked(part_of(qkvf_ref, 0, g)), part_of(qkvf_ref, 1, g)), vis)

    def scores(g, affinity):
        lanes = lanes_of(g)
        numer = select(dot(affinity, slots[:, lanes]))
        numer = numer + carried * dot_nt(part_of(qkvf_ref, 0, g), key_states[g])
        inverse = 1.0 / (norm[:, lanes] + carried * norm_state[:, lanes])
        return numer * inverse * SCALE, inverse

    def grow(score):
        return jnp.exp(score - head_max(score))

    def read(g, score, inverse, grown):
        lanes = lanes_of(g)
        probs = grown / head_sums(grown)
        p_ref[:, lanes] = probs
        s_ref[:, lanes] = score
        z_ref[:, lanes] = inverse
        return (probs * inverse).astype(BF16)

    def mixing(g, reading):
        return masked(dot_nt(stacked(reading), slots[:, lanes_of(g)]), vis)

    def mixed(g, reading, mix):
        out = select(dot(mix, part_of(qkvf_ref, 2, g))) + carried * dot(reading, value_states[g])
        o_ref[:, lanes_of(g)] = out.astype(BF16)

    affinity = affine(0)
    score, inverse = scores(0, affinity)
    affinity = affine(1)
    grown = grow(score)
    score_two, inverse_two = scores(1, affinity)
    reading = read(0, score, inverse, grown)
    tail = wide(flag(col, newest), 4).astype(BF16) * slots
    new_keys, new_values = state_terms(tail, qkvf_ref[:, D : 2 * D], qkvf_ref[:, 2 * D : 3 * D])
    same = jnp.where(last == newest, 1.0, 0.0)
    state[0:64] = same * state[0:64] + new_keys
    state[64:128] = same * state[64:128] + new_values
    state[128:129] = same * state[128:129] + jnp.sum(tail.astype(F32), axis=0, keepdims=True)
    grown = grow(score_two)
    mix = mixing(0, reading)
    reading_two = read(1, score_two, inverse_two, grown)
    mixed(0, reading, mix)
    mix = mixing(1, reading_two)
    mixed(1, reading_two, mix)


MESH_ID = pl.DeviceIdType.MESH


def places():
    seq, at = lax.axis_index("seq"), lax.axis_index("fsdp")
    core = lax.rem(seq, 2)
    return seq, at, seq + 1 - 2 * core, lax.rem(seq + 2, 4)


def push(src, dst, send, recv, **device):
    return pltpu.make_async_remote_copy(
        src_ref=src, dst_ref=dst, send_sem=send, recv_sem=recv,
        device_id=device, device_id_type=MESH_ID,
    )


def greet(count):
    seq, at, _, _ = places()
    barrier = pltpu.get_barrier_semaphore()
    for k in range(1, count):
        pl.semaphore_signal(barrier, inc=1, device_id={"fsdp": at ^ k}, device_id_type=MESH_ID)
    for k in range(1, 4):
        pl.semaphore_signal(barrier, inc=1, device_id={"seq": seq ^ k}, device_id_type=MESH_ID)


def met(count):
    pl.semaphore_wait(pltpu.get_barrier_semaphore(), count - 1 + 3)


class Gather:
    def __init__(self, count, mine, held, base, width, four, sems):
        self.count, self.mine, self.held, self.four = count, mine, held, four
        self.far, self.near, self.core, self.chip, self.onward, self.local = sems
        self.seq, self.at, self.sibling, self.beside = places()
        self.base, self.share = base, width // (4 if four else 2)
        self.evens = range(0, count, 2)

    def lanes(self, seq):
        place = seq if self.four else lax.rem(seq, 2)
        return pl.ds(pl.multiple_of(self.base + place * self.share, 128), self.share)

    def part(self, k, seq):
        return self.held.at[self.at ^ k, :, self.lanes(seq)]

    def source(self, k):
        if k:
            return self.part(k, self.seq)
        return self.mine.at[:, self.lanes(self.seq)]

    def own(self):
        return pltpu.make_async_copy(self.source(0), self.part(0, self.seq), self.local)

    def over(self, sems, k, **device):
        return push(self.source(k), self.part(k, self.seq), sems[0].at[k], sems[1].at[k], **device)

    def come(self, sems, k, owner):
        here = self.part(owner, self.seq)
        return push(here, here, sems[0].at[k], sems[1].at[k], seq=self.sibling)

    def far_out(self, k):
        return push(
            self.source(0), self.part(0, self.seq), self.far[0].at[k], self.far[1].at[k],
            fsdp=self.at ^ k,
        )

    def far_in(self, k):
        return self.come(self.far, k, k)

    def near_out(self, k):
        return self.over(self.near, k, fsdp=self.at ^ 1)

    def near_in(self, k):
        return self.come(self.near, k, k ^ 1)

    def start(self):
        self.own().start()
        for k in self.evens[1:]:
            self.far_out(k).start()
        self.near_out(0).start()

    def second(self):
        for k in self.evens[1:]:
            self.far_in(k).wait_recv()
            self.near_out(k).start()

    def hop(self, sems, source, target):
        here = self.held.at[:, :, self.lanes(source)]
        return push(here, here, sems[0].at[0], sems[1].at[0], seq=target)

    def third(self):
        self.own().wait()
        for k in self.evens:
            self.near_in(k).wait_recv()
        self.hop(self.core, self.seq, self.sibling).start()
        if self.four:
            self.hop(self.chip, self.seq, self.beside).start()

    def fourth(self):
        self.hop(self.chip, self.beside, self.beside).wait_recv()
        self.hop(self.onward, self.beside, self.sibling).start()

    def finish(self):
        self.hop(self.core, self.sibling, self.sibling).wait_recv()
        self.hop(self.core, self.seq, self.sibling).wait_send()
        if self.four:
            self.hop(self.onward, lax.rem(self.sibling + 2, 4), self.sibling).wait_recv()
            self.hop(self.chip, self.seq, self.beside).wait_send()
            self.hop(self.onward, self.beside, self.sibling).wait_send()

    def core_out(self, k):
        return self.over(self.core, k, seq=self.sibling)

    def core_in(self, k):
        here = self.part(k, self.sibling)
        return push(here, here, self.core[0].at[k], self.core[1].at[k], seq=self.sibling)

    def at_once(self, between):
        self.start()
        self.core_out(0).start()
        for k in self.evens[1:]:
            self.far_in(k).wait_recv()
            self.near_out(k).start()
            self.core_out(k).start()
        between()
        for k in self.evens:
            self.near_in(k).wait_recv()
            self.core_out(k ^ 1).start()
        self.own().wait()
        for k in range(self.count):
            self.core_in(k).wait_recv()

    def drain(self, each=False):
        for k in self.evens:
            self.near_out(k).wait_send()
            if k:
                self.far_out(k).wait_send()
        if each:
            for k in range(self.count):
                self.core_out(k).wait_send()


def gather_sems(count, each):
    n = count if each else 1
    pair = lambda size: [pltpu.SemaphoreType.DMA((size,)), pltpu.SemaphoreType.DMA((size,))]
    return pair(count) + pair(count) + pair(n) + pair(1) + pair(1) + [pltpu.SemaphoreType.DMA]


def bundle(refs):
    return [(refs[2 * n], refs[2 * n + 1]) for n in range(5)] + [refs[10]]


class States:
    def __init__(self, big, small, sems):
        self.refs, self.sems = (big, small), sems
        self.seq, _, self.sibling, self.beside = places()

    def hop(self, n, source, target):
        out = []
        for m, ref in enumerate(self.refs):
            here = ref.at[source]
            out.append(push(here, here, self.sems[0].at[n, m], self.sems[1].at[n, m], seq=target))
        return out

    def start(self):
        for copy in self.hop(0, self.seq, self.sibling) + self.hop(1, self.seq, self.beside):
            copy.start()

    def finish(self):
        for copy in self.hop(1, self.beside, self.beside):
            copy.wait_recv()
        for copy in self.hop(2, self.beside, self.sibling):
            copy.start()
        for copy in self.hop(0, self.sibling, self.sibling):
            copy.wait_recv()
        for copy in self.hop(2, lax.rem(self.sibling + 2, 4), self.sibling):
            copy.wait_recv()

    def drain(self):
        for copy in (
            self.hop(0, self.seq, self.sibling)
            + self.hop(1, self.seq, self.beside)
            + self.hop(2, self.beside, self.sibling)
        ):
            copy.wait_send()


def doc_parts(doc_ref, col_ref, edge_ref):
    here = lax.broadcasted_iota(jnp.int32, (C, C), 0)
    there = lax.broadcasted_iota(jnp.int32, (C, C), 1)
    eye = jnp.where(here == there, 1.0, 0.0).astype(BF16)
    for n in range(doc_ref.shape[1] // C):
        row = doc_ref[:, n * C : (n + 1) * C].astype(F32)
        col_ref[n * C : (n + 1) * C] = dot_nt(eye, jnp.broadcast_to(row, (128, C)).astype(BF16))
        low = jnp.min(row, axis=1, keepdims=True)
        high = jnp.max(row, axis=1, keepdims=True)
        edge_ref[n : n + 1] = jnp.broadcast_to(low, (1, D))
        edge_ref[n + 8 : n + 9] = jnp.broadcast_to(high, (1, D))


def spread_small(vec_refs, bias_ref, out_ref):
    def repeat(values):
        width = values.shape[1]
        rows = lax.broadcasted_iota(jnp.int32, (width, 128), 0)
        lanes = lax.broadcasted_iota(jnp.int32, (width, 128), 1)
        pick = jnp.where(lax.rem(lanes, width) == rows, 1.0, 0.0).astype(BF16)
        return dot(jnp.broadcast_to(values, (8, width)).astype(BF16), pick)[0:1]

    out_ref[...] = jnp.zeros_like(out_ref)
    for n, ref in enumerate(vec_refs):
        out_ref[n : n + 1] = repeat(ref[...])
    for b in range(max(bias_ref.shape[1] // 128, 1)):
        out_ref[5 + b : 6 + b] = repeat(bias_ref[:, b * 128 : (b + 1) * 128])


def join_small(count, part, gathered, vec_ref, bias_ref):
    lanes = lax.broadcasted_iota(jnp.int32, (8, D), 1)
    total = jnp.zeros((8, D), F32)
    for f in range(count):
        total = jnp.where(lanes // part == f, wide(gathered[f], 4), total)
    vec_ref[...] = total
    size = 4 * part
    for r in range(4):
        at = lanes[0:1] + r * D
        row = jnp.zeros((1, D), F32)
        for f in range(r * D // size, -(-(r + 1) * D // size)):
            for b in range(max(size // 128, 1)):
                use = (at // size == f) & (lax.rem(at, size) // 128 == b)
                row = jnp.where(use, wide(gathered[f, 5 + b : 6 + b], 4), row)
        bias_ref[0:1, r * D : (r + 1) * D] = row


ROOT = 0.7978845608028654
CUBE = 0.044715


def gelu_both(u):
    square = u * u
    bent = jnp.tanh(ROOT * u * (1.0 + CUBE * square))
    half = 0.5 * (1.0 + bent)
    slope = half + 0.5 * u * (1.0 - bent * bent) * (ROOT * (1.0 + 3.0 * CUBE * square))
    return u * half, slope


def feed_body(
    values, attended, cot, vec_ref, bias_ref, w_out, w_hidden, w_return, ready,
    y_ref, dy_ref, do_ref, gsmall_ref, gwo_ref, gwh_ref, gwr_ref,
):
    middle = values.astype(F32) + dot(attended, w_out())
    unit, scale = norm_parts(middle)
    hidden = (unit * vec_ref[2:3] + vec_ref[3:4]).astype(BF16)
    out = middle + vec_ref[4:5]
    grad_hidden = jnp.zeros_like(middle)
    cot32 = cot.astype(F32)
    tiles = FF // FEED_LANES
    ready()

    def into(j):
        cols = slice(j * FEED_LANES, (j + 1) * FEED_LANES)
        inner = dot(hidden, w_hidden(j)) + bias_ref[0:1, cols]
        return inner, dot_nt(cot, w_return(j))

    def bend(inner, grad):
        gated, slope = gelu_both(inner)
        return gated.astype(BF16), (grad * slope).astype(BF16)

    def outof(j, active, low):
        cols = slice(j * FEED_LANES, (j + 1) * FEED_LANES)
        there = slice(cols.start % D, cols.start % D + FEED_LANES)
        row = 8 + cols.start // D
        gwr_ref[:, cols] += dot_tn(cot, active)
        gsmall_ref[row : row + 1, there] += jnp.sum(low.astype(F32), axis=0, keepdims=True)
        gwh_ref[:, cols] += dot_tn(hidden, low)
        return dot(active, w_return(j)), dot_nt(low, w_hidden(j))

    coming = into(0)
    for j in range(tiles):
        bent = bend(*coming)
        if j + 1 < tiles:
            coming = into(j + 1)
        to_out, to_hidden = outof(j, *bent)
        out = out + to_out
        grad_hidden = grad_hidden + to_hidden
    y_ref[...] = out.astype(BF16)
    gsmall_ref[2:3] += jnp.sum(grad_hidden * unit, axis=0, keepdims=True)
    gsmall_ref[3:4] += jnp.sum(grad_hidden, axis=0, keepdims=True)
    gsmall_ref[4:5] += jnp.sum(cot32, axis=0, keepdims=True)
    grad_middle = cot32 + norm_back(unit, scale, vec_ref[2:3], grad_hidden)
    dy_ref[...] = grad_middle
    branch = grad_middle.astype(BF16)
    gwo_ref[...] += dot_tn(attended, branch)
    do_ref[...] = dot_nt(branch, w_out()).astype(BF16)


def pack_grads(count, part, gwo_ref, gwh_ref, gwr_ref, put):
    half = count // 2
    for q in range(4):
        x, c = q // 2, q % 2
        hidden_part = gwh_ref[:, q * 512 : (q + 1) * 512].reshape(half, 2, part, 512)
        out_part = gwo_ref[:, q * 128 : (q + 1) * 128].reshape(half, 2, part, 128)
        turned = gwr_ref[q * 128 : (q + 1) * 128].T.reshape(half, 2, 4, part, 128)
        for y in range(2):
            over_x, over_y = ((c * 2 + x) * 2 + y) * half, ((c * 2 + y) * 2 + x) * half
            put(0, over_x, slice(0, 512), hidden_part[:, y])
            put(0, over_x, slice(512, 640), out_part[:, y])
            for j in range(4):
                put(1, over_y, slice(j * 128, (j + 1) * 128), turned[:, y, j])


def feed_kernel(
    x_ref, o_ref, g_ref, small_ref, bias_ref, wo_ref, wh_ref, wr_ref,
    y_ref, dy_ref, do_ref, pack_ref, pack_r_ref, gsmall_ref, gwo_ref, gwh_ref, gwr_ref,
):
    step = pl.program_id(0)
    count, part = wh_ref.shape[0], wh_ref.shape[1]

    @pl.when(step == 0)
    def _():
        for ref in (gwo_ref, gwh_ref, gwr_ref, gsmall_ref):
            ref[...] = jnp.zeros_like(ref)

    feed_body(
        x_ref[...], o_ref[...], g_ref[...], small_ref, bias_ref, *weight_views(wo_ref, wh_ref, wr_ref),
        lambda: None, y_ref, dy_ref, do_ref, gsmall_ref, gwo_ref, gwh_ref, gwr_ref,
    )

    @pl.when(step == pl.num_programs(0) - 1)
    def _():
        def put(which, slab, lanes, values):
            ref = (pack_ref, pack_r_ref)[which]
            n = values.shape[0] * part
            ref[slab * part : slab * part + n, lanes] = values.reshape(n, -1).astype(ref.dtype)

        pack_grads(count, part, gwo_ref, gwh_ref, gwr_ref, put)


def weight_views(wo_ref, wh_ref, wr_ref):
    def w_out():
        return wo_ref[...].reshape(D, D).astype(BF16)

    def w_hidden(j):
        cols = slice(j * FEED_LANES, (j + 1) * FEED_LANES)
        return wh_ref[:, :, cols].reshape(D, FEED_LANES).astype(BF16)

    def w_return(j):
        n = FEED_LANES // wr_ref.shape[1]
        return wr_ref[j * n : (j + 1) * n].reshape(FEED_LANES, D).astype(BF16)

    return w_out, w_hidden, w_return


def front_kernel(count, joined, names, *refs):
    r = types.SimpleNamespace(**dict(zip(names, refs)))
    sems = refs[len(names) :]
    x_ref, doc_ref, vec_out, bias_out = r.x, r.doc, r.vec, r.bias
    qkvf, hidden, w_all, mine = r.qkvf, r.hidden, r.w_all, r.mine
    mine_o, mine_h, mine_r, spread, smalls = r.mine_o, r.mine_h, r.mine_r, r.spread, r.smalls
    col_ref, edge_ref, state, tail = r.col, r.edge, r.state, r.tail
    tails, tail_rows = r.tails, r.tail_rows
    step = pl.program_id(0)
    seq, at, _, _ = places()
    link = mine.dtype
    groups_of_sems = []
    for _ in range(5):
        groups_of_sems.append(bundle(sems[:11]))
        sems = sems[11:]
    small_send, small_recv, state_send, state_recv, out_sem, stage_sem, fed_sem = sems
    main = Gather(count, mine, w_all, D, 3 * D, False, groups_of_sems[0])
    q_piece = Gather(count, mine, w_all, 0, D, False, groups_of_sems[1])
    o_piece = Gather(count, mine_o, r.wo_all, 0, D, True, groups_of_sems[2])
    h_piece = Gather(count, mine_h, r.wh_all, 0, FF, True, groups_of_sems[3])
    r_piece = Gather(count, mine_r, r.wr_all, 0, D, False, groups_of_sems[4])
    later = (q_piece, o_piece, h_piece, r_piece)
    states = States(tails, tail_rows, (state_send, state_recv))

    def small_copy(k, owner):
        return push(
            spread, smalls.at[owner], small_send.at[k], small_recv.at[k], fsdp=at ^ k
        )

    def save():
        return (
            pltpu.make_async_copy(qkvf, r.qkvf_out, out_sem.at[0]),
            pltpu.make_async_copy(w_all, r.w_out, out_sem.at[1]),
        )

    @pl.when(step == 0)
    def _():
        greet(count)
        for n, ref in enumerate((r.w0, r.w1, r.w2, r.w3)):
            mine[:, n * D : (n + 1) * D] = ref[...].astype(BF16).astype(link)
        spread_small((r.v0, r.v1, r.v2, r.v3, r.v4), r.bias_in, spread)
        doc_parts(doc_ref, col_ref, edge_ref)
        tail[...] = jnp.zeros_like(tail)
        met(count)
        for k in range(1, count):
            small_copy(k, at).start()

        def between():
            mine_o[...] = r.w4[...].astype(BF16).astype(link)
            mine_h[...] = r.w5[...].astype(BF16).astype(link)
            mine_r[...] = r.w6[...].astype(BF16).astype(link)
            smalls[at] = spread[...]
            for k in range(1, count):
                small_copy(k, at ^ k).wait_recv()
            join_small(count, r.v0.shape[1], smalls, vec_out, bias_out)
            q_piece.start()
            o_piece.start()

            @pl.loop(0, 8)
            def _(n):
                here = pl.ds(pl.multiple_of(n * C, C), C)
                unit, _ = norm_parts(x_ref[here].astype(F32))
                hidden[here] = (unit * vec_out[0:1] + vec_out[1:2]).astype(BF16)

        main.at_once(between)
        h_piece.start()
        r_piece.start()

    @pl.when(step < FRONT)
    def _():
        size = 8 // FRONT * C
        here = pl.ds(pl.multiple_of(step * size, size), size)
        weights = w_all[:, :, D:].reshape(D, 3 * D).astype(BF16)
        rows = dot(hidden[here], weights).astype(BF16)
        qkvf[here, D:] = rows
        slots = wide(flag(col_ref[here], edge_ref[15:16]), 4) * jnp.exp(rows[:, 2 * D :].astype(F32))
        slots = slots.astype(BF16)
        keys, values = state_terms(slots, rows[:, 0:D], rows[:, D : 2 * D])
        tail[0:64] += keys
        tail[64:128] += values
        tail[128:129] += jnp.sum(slots.astype(F32), axis=0, keepdims=True)

    @pl.when(step == 1)
    def _():
        q_piece.second()
        o_piece.second()

    @pl.when(step == FRONT - 1)
    def _():
        tails[seq] = tail[0:128].astype(link)
        tail_rows[seq, 0:1] = tail[128:129]
        tail_rows[seq, 1:2] = edge_ref[15:16]
        tail_rows[seq, 2:8] = jnp.zeros((6, D), F32)
        states.start()
        q_piece.third()
        q_piece.finish()

        @pl.loop(0, FRONT)
        def _(n):
            size = 8 // FRONT * C
            here = pl.ds(pl.multiple_of(n * size, size), size)
            weights = w_all[:, :, 0:D].reshape(D, D).astype(BF16)
            qkvf[here, 0:D] = dot(hidden[here], weights).astype(BF16)

        for copy in save():
            copy.start()
        o_piece.third()

        @pl.loop(0, 8)
        def _(n):
            here = pl.ds(pl.multiple_of(n * C, C), C)
            hidden[here] = jnp.exp(qkvf[here, 3 * D :].astype(F32)).astype(BF16)
            r.seen[n] = visible(col_ref[here], doc_ref[:, here].astype(F32))

        states.finish()
        first = edge_ref[0:1]
        state[...] = jnp.zeros_like(state)
        for n in range(4):
            use = jnp.where(tail_rows[n, 1:2] == first, 1.0, 0.0) * (n < seq).astype(F32)
            state[0:128] += use * tails[n].astype(F32)
            state[128:129] += use * tail_rows[n, 0:1]
        h_piece.second()

    per = 8 // FRONT

    def kept_copies(n):
        here = pl.ds(pl.multiple_of(n * per * C, per * C), per * C)
        slot = lax.rem(n, 2)
        return [
            pltpu.make_async_copy(r.stage.at[slot, k], out.at[here], stage_sem.at[slot, k])
            for k, out in enumerate((r.p, r.s, r.z))
        ]

    @pl.when((step >= FRONT + 2) & (step < 2 * FRONT))
    def _():
        for copy in kept_copies(step - FRONT - 2):
            copy.wait()

    @pl.when((step >= FRONT) & (step < 2 * FRONT))
    def _():
        slot = lax.rem(step - FRONT, 2)

        @pl.loop(0, per)
        def _(u):
            n = (step - FRONT) * per + u
            here = pl.ds(pl.multiple_of(n * C, C), C)
            block = pl.ds(pl.multiple_of(u * C, C), C)
            attend_body(
                n, qkvf.at[here], hidden[here], r.seen[n], col_ref[here], edge_ref, state,
                r.o.at[here if joined else block], *(r.stage.at[slot, k, block] for k in range(3)),
                r.kept.at[pl.ds(u, 1)],
            )

            @pl.when(n == 0)
            def _():
                o_piece.fourth()

            @pl.when(n == per - 1)
            def _():
                r_piece.second()

            @pl.when(n == per)
            def _():
                h_piece.third()

    @pl.when((step >= FRONT) & (step < 2 * FRONT))
    def _():
        for copy in kept_copies(step - FRONT):
            copy.start()

    @pl.when(step == 2 * FRONT - 1)
    def _():
        r_piece.third()
        h_piece.fourth()
        o_piece.finish()
        for copy in save():
            copy.wait()

    def complete():
        h_piece.finish()
        r_piece.finish()
        for piece in later:
            piece.drain()
        main.drain(True)
        states.drain()
        for k in range(1, count):
            small_copy(k, at).wait_send()
        for n in (FRONT - 2, FRONT - 1):
            for copy in kept_copies(n):
                copy.wait()

    if not joined:
        pl.when(step == 2 * FRONT - 1)(complete)
        return

    @pl.when(step == 2 * FRONT)
    def _():
        for ref in (r.gwo, r.gwh, r.gwr, r.gsmall):
            ref[...] = jnp.zeros_like(ref)

    fed = step - 2 * FRONT

    def fed_copies(n):
        here = pl.ds(pl.multiple_of(n * FEED_ROWS, FEED_ROWS), FEED_ROWS)
        slot = lax.rem(n, 2)
        pairs = ((r.held_y, r.y), (r.held_dy, r.dy), (r.held_do, r.do))
        return [
            pltpu.make_async_copy(held.at[slot], out.at[here], fed_sem.at[slot, k])
            for k, (held, out) in enumerate(pairs)
        ]

    @pl.when(fed >= 2)
    def _():
        for copy in fed_copies(fed - 2):
            copy.wait()

    @pl.when(fed >= 0)
    def _():
        here = pl.ds(pl.multiple_of(fed * FEED_ROWS, FEED_ROWS), FEED_ROWS)
        slot = lax.rem(fed, 2)
        feed_body(
            x_ref[here], r.o[here], r.g[...], vec_out, bias_out,
            *weight_views(r.wo_all, r.wh_all, r.wr_all),
            lambda: pl.when(step == 2 * FRONT)(complete),
            r.held_y.at[slot], r.held_dy.at[slot], r.held_do.at[slot], r.gsmall, r.gwo, r.gwh, r.gwr,
        )
        for copy in fed_copies(fed):
            copy.start()

    @pl.when(step == pl.num_programs(0) - 1)
    def _():
        part = mine.shape[0]

        def put(which, slab, lanes, values):
            n = values.shape[0] * part
            at_lane = 640 * which + lanes.start
            qkvf[slab * part : slab * part + n, at_lane : at_lane + values.shape[2]] = (
                values.reshape(n, -1).astype(BF16)
            )

        pack_grads(count, part, r.gwo, r.gwh, r.gwr, put)
        copies = [
            pltpu.make_async_copy(qkvf.at[:, 0:640], r.pack, out_sem.at[0]),
            pltpu.make_async_copy(qkvf.at[:, 640:1152], r.pack_r, out_sem.at[1]),
        ]
        for copy in copies:
            copy.start()
        last = x_ref.shape[0] // FEED_ROWS - 1
        for copy in (*fed_copies(last - 1), *fed_copies(last), *copies):
            copy.wait()


def front(count, tokens, doc_ids, weights, vectors, bias, cotangent):
    rows = tokens.shape[0]
    part = weights[0].shape[0]
    link = BF16 if part % 16 == 0 else F32
    joined = link == BF16
    per = 8 // FRONT
    once = lambda a: pl.BlockSpec(a.shape, lambda i: (0,) * a.ndim)
    late = lambda i: jnp.clip(i - FRONT, 0, FRONT - 1)
    tall = pl.BlockSpec((per * C, D), lambda i: (late(i), 0))
    fed = pl.BlockSpec((FEED_ROWS, D), lambda i: (jnp.maximum(i - 2 * FRONT, 0), 0))
    anywhere = pl.BlockSpec(memory_space=pl.ANY)
    vmem, dma = pltpu.VMEM, pltpu.SemaphoreType.DMA
    ins = {"x": (tokens, once(tokens)), "doc": (doc_ids, once(doc_ids))}
    ins |= {f"w{n}": (a, once(a)) for n, a in enumerate(weights)}
    ins |= {f"v{n}": (a, once(a)) for n, a in enumerate(vectors)}
    ins["bias_in"] = (bias, once(bias))
    wide_rows, slabs = shape_of((rows, D), F32), 4 * count
    outs = {
        "qkvf_out": (shape_of((rows, 4 * D), BF16), anywhere),
        "p": (wide_rows, anywhere),
        "s": (wide_rows, anywhere),
        "z": (wide_rows, anywhere),
        "kept": (
            shape_of((8, 128, D), F32), pl.BlockSpec((per, 128, D), lambda i: (late(i), 0, 0)),
        ),
        "w_out": (shape_of((count, part, 4 * D), link), anywhere),
        "vec": (shape_of((8, D), F32), whole(8, D)),
    }
    scratch = {
        "qkvf": vmem((rows, 4 * D), BF16),
        "hidden": vmem((rows, D), BF16),
        "w_all": vmem((count, part, 4 * D), link),
        "mine": vmem((part, 4 * D), link),
        "mine_o": vmem((part, D), link),
        "mine_h": vmem((part, FF), link),
        "mine_r": vmem((4 * part, D), link),
        "spread": vmem((8, 128), F32),
        "smalls": vmem((count, 8, 128), F32),
        "col": vmem((rows, 128), F32),
        "edge": vmem((16, D), F32),
        "state": vmem((136, D), F32),
        "tail": vmem((136, D), F32),
        "tails": vmem((4, 128, D), link),
        "tail_rows": vmem((4, 8, D), F32),
        "stage": vmem((2, 3, per * C, D), F32),
        "seen": vmem((8, C, C), BF16),
    }
    gathered = {
        "wo_all": (count, part, D), "wh_all": (count, part, FF), "wr_all": (count, 4 * part, D),
    }
    if joined:
        ins["g"] = (cotangent, fed)
        outs |= {
            "y": (shape_of((rows, D), BF16), anywhere),
            "dy": (wide_rows, anywhere),
            "do": (shape_of((rows, D), BF16), anywhere),
            "pack": (shape_of((slabs * part, 640), BF16), anywhere),
            "pack_r": (shape_of((slabs * part, D), BF16), anywhere),
            "gsmall": (shape_of((16, D), F32), whole(16, D)),
        }
        scratch |= {name: vmem(shape, link) for name, shape in gathered.items()}
        scratch |= {
            "held_y": vmem((2, FEED_ROWS, D), BF16), "held_dy": vmem((2, FEED_ROWS, D), F32),
            "held_do": vmem((2, FEED_ROWS, D), BF16),
            "o": vmem((rows, D), BF16), "bias": vmem((1, FF), F32), "gwo": vmem((D, D), F32),
            "gwh": vmem((D, FF), F32), "gwr": vmem((D, FF), F32),
        }
    else:
        outs |= {name: (shape_of(shape, link), anywhere) for name, shape in gathered.items()}
        outs |= {
            "o": (shape_of((rows, D), BF16), tall), "bias": (shape_of((1, FF), F32), whole(1, FF)),
        }
    found = pl.pallas_call(
        functools.partial(front_kernel, count, joined, (*ins, *outs, *scratch)),
        grid=(2 * FRONT + (rows // FEED_ROWS if joined else 0),),
        in_specs=[spec for _, spec in ins.values()],
        out_specs=[spec for _, spec in outs.values()],
        out_shape=[shape for shape, _ in outs.values()],
        scratch_shapes=list(scratch.values())
        + gather_sems(count, True)
        + gather_sems(count, False) * 4
        + [dma((count,)), dma((count,)), dma((3, 2)), dma((3, 2)), dma((2,)), dma((2, 3)), dma((2, 3))],
        compiler_params=pltpu.CompilerParams(
            vmem_limit_bytes=62 * MIB, collective_id=1, has_side_effects=True
        ),
        name="front",
    )(*(a for a, _ in ins.values()))
    found = dict(zip(outs, found))
    if not joined:
        found |= feed(count, part, tokens, found, cotangent, link)
    return found


def feed(count, part, tokens, found, cotangent, link):
    rows, slabs = tokens.shape[0], 4 * count
    tall = pl.BlockSpec((256, D), lambda i: (i, 0))
    weights = [found[name] for name in ("wo_all", "wh_all", "wr_all")]
    names = ("y", "dy", "do", "pack", "pack_r", "gsmall")
    return dict(
        zip(
            names,
            pl.pallas_call(
                feed_kernel,
                grid=(rows // 256,),
                in_specs=[tall] * 3
                + [whole(8, D), whole(1, FF)]
                + [whole(*a.shape) for a in weights],
                out_specs=[tall] * 3
                + [whole(slabs * part, 640), whole(slabs * part, D), whole(16, D)],
                out_shape=[
                    shape_of((rows, D), BF16),
                    shape_of((rows, D), F32),
                    shape_of((rows, D), BF16),
                    shape_of((slabs * part, 640), link),
                    shape_of((slabs * part, D), link),
                    shape_of((16, D), F32),
                ],
                scratch_shapes=[
                    pltpu.VMEM((D, D), F32), pltpu.VMEM((D, FF), F32), pltpu.VMEM((D, FF), F32),
                ],
                compiler_params=PARAMS,
                name="feed",
            )(tokens, found["o"], cotangent, found["vec"], found["bias"], *weights),
        )
    )


def row_body(
    n, qkvf_ref, do_ref, p_ref, s_ref, z_ref, kept_ref, col, row, edge_ref,
    r_ref, dn_ref, dz_ref, head_ref, aside,
):
    first = edge_ref[pl.ds(0, 1)]
    before = edge_ref[pl.ds(8 + jnp.maximum(n - 1, 0), 1)]
    last = jnp.where(n == 0, first, before)
    vis = visible(col, row)
    carried = wide(flag(col, last), 2)
    slots = jnp.exp(qkvf_ref[:, 3 * D :].astype(F32)).astype(BF16)
    own = wide(flag(col, first), 2)
    states = [expand(kept_ref[0, 64:128, lanes_of(g)]).astype(BF16) for g in range(2)]

    def mixing(g):
        return masked(dot_nt(stacked(do_ref[:, lanes_of(g)]), part_of(qkvf_ref, 2, g)), vis)

    def to_reading(g, back_mix):
        lanes = lanes_of(g)
        back = select(dot(back_mix, slots[:, lanes]))
        return back + carried * dot_nt(do_ref[:, lanes], states[g])

    def to_scores(g, back_reading):
        lanes = lanes_of(g)
        probs, score, inverse = p_ref[:, lanes], s_ref[:, lanes], z_ref[:, lanes]
        shared = back_reading * inverse * probs
        back_score = shared - probs * head_sums(shared)
        back_numer = back_score * inverse * SCALE
        back_total = -(shared + back_score * score) * inverse
        reading = (probs * inverse).astype(BF16)
        r_ref[:, lanes] = reading
        dn_ref[:, lanes] = back_numer
        dz_ref[:, lanes] = back_total
        return back_numer, back_total, reading

    def to_state(g, back_numer, back_total, reading):
        lanes = lanes_of(g)
        head_ref[0:64, lanes] += compacted(
            dot_tn((own * back_numer).astype(BF16), part_of(qkvf_ref, 0, g))
        )
        head_ref[64:128, lanes] += compacted(
            dot_tn((own * reading.astype(F32)).astype(BF16), do_ref[:, lanes])
        )
        head_ref[128:129, lanes] += jnp.sum(own * back_total, axis=0, keepdims=True)

    back_mix = mixing(0)
    back_mix_two = mixing(1)
    aside()
    back_reading = to_reading(0, back_mix)
    back_reading_two = to_reading(1, back_mix_two)
    parts = to_scores(0, back_reading)
    to_state(0, *parts)
    parts = to_scores(1, back_reading_two)
    to_state(1, *parts)


def query_body(n, qkvf_ref, kept_ref, col, row, edge_ref, dn_ref, dq_ref):
    first = edge_ref[pl.ds(0, 1)]
    before = edge_ref[pl.ds(8 + jnp.maximum(n - 1, 0), 1)]
    last = jnp.where(n == 0, first, before)
    vis = visible(col, row)
    carried = wide(flag(col, last), 2)
    slots = jnp.exp(qkvf_ref[:, 3 * D :].astype(F32)).astype(BF16)
    lows = [dn_ref[:, lanes_of(g)].astype(BF16) for g in range(2)]
    states = [expand(kept_ref[0, 0:64, lanes_of(g)]).astype(BF16) for g in range(2)]

    def affine(g):
        return masked(dot_nt(stacked(lows[g]), slots[:, lanes_of(g)]), vis)

    def to_queries(g, back_affinity):
        out = select(dot(back_affinity, part_of(qkvf_ref, 1, g))) + carried * dot(lows[g], states[g])
        dq_ref[:, lanes_of(g)] = out.astype(BF16)

    one, two = affine(0), affine(1)
    to_queries(0, one)
    to_queries(1, two)


def column_body(
    n, qkvf_ref, do_ref, r_ref, dn_ref, dz_ref, col, row, edge_ref, state, snap, snap_rows, d_ref
):
    newest = edge_ref[15:16]
    after = edge_ref[pl.ds(jnp.minimum(n + 1, 7), 1)]
    following = jnp.where(n == 7, newest, after)
    first = edge_ref[pl.ds(n, 1)]
    vis = visible_back(col, row)
    carried = wide(flag(col, following), 2)
    own = wide(flag(col, first), 2)
    kept = jnp.where(following == first, 1.0, 0.0)[:, :GROUP]
    snap[n] = state[0:128].astype(BF16)
    snap_rows[pl.ds(n, 1)] = state[128:129]
    key_states = [expand(state[0:64, lanes_of(g)]).astype(BF16) for g in range(2)]
    value_states = [expand(state[64:128, lanes_of(g)]).astype(BF16) for g in range(2)]
    slots = jnp.exp(qkvf_ref[:, 3 * D :].astype(F32)).astype(BF16)
    numers = [dn_ref[:, lanes_of(g)] for g in range(2)]

    def mixing(g, apart):
        return masked(dot_nt(apart, r_ref[:, lanes_of(g)]), vis)

    def affine(g, apart):
        return masked(dot_nt(apart, numers[g].astype(BF16)), vis)

    def to_values(g, mix):
        lanes = lanes_of(g)
        out = select(dot(mix, do_ref[:, lanes])) + carried * dot(slots[:, lanes], value_states[g])
        d_ref[:, 2 * D + g * GROUP : 2 * D + (g + 1) * GROUP] = out.astype(BF16)

    def to_keys(g, back_affinity):
        lanes = lanes_of(g)
        out = select(dot(back_affinity, part_of(qkvf_ref, 0, g)))
        out = out + carried * dot(slots[:, lanes], key_states[g])
        d_ref[:, D + g * GROUP : D + (g + 1) * GROUP] = out.astype(BF16)

    def to_state(g):
        lanes = lanes_of(g)
        state[0:64, lanes] = kept * state[0:64, lanes] + compacted(
            dot_tn((own * numers[g]).astype(BF16), part_of(qkvf_ref, 0, g))
        )
        state[64:128, lanes] = kept * state[64:128, lanes] + compacted(
            dot_tn((own * r_ref[:, lanes].astype(F32)).astype(BF16), do_ref[:, lanes])
        )
        state[128:129, lanes] = kept * state[128:129, lanes] + jnp.sum(
            own * dz_ref[:, lanes], axis=0, keepdims=True
        )

    apart = stacked(slots[:, lanes_of(0)])
    mix = mixing(0, apart)
    back_affinity = affine(0, apart)
    apart = stacked(slots[:, lanes_of(1)])
    mix_two = mixing(1, apart)
    to_values(0, mix)
    affinity_two = affine(1, apart)
    to_keys(0, back_affinity)
    to_state(0)
    to_values(1, mix_two)
    to_keys(1, affinity_two)
    to_state(1)


def slot_body(n, qkvf_ref, do_ref, r_ref, dn_ref, dz_ref, col, row, edge_ref, snap, snap_rows, d_ref):
    newest = edge_ref[15:16]
    after = edge_ref[pl.ds(jnp.minimum(n + 1, 7), 1)]
    following = jnp.where(n == 7, newest, after)
    vis = visible_back(col, row)
    carried = wide(flag(col, following), 2)
    left = lane_heads(C, 128) == 0
    norm_state = snap_rows[pl.ds(n, 1)]
    key_states = [expand(snap[n, 0:64, lanes_of(g)]) for g in range(2)]
    value_states = [expand(snap[n, 64:128, lanes_of(g)]) for g in range(2)]

    def mixing(g):
        return masked(dot_nt(stacked(part_of(qkvf_ref, 2, g)), do_ref[:, lanes_of(g)]), vis)

    def affine(g):
        return masked(dot_nt(stacked(part_of(qkvf_ref, 1, g)), part_of(qkvf_ref, 0, g)), vis)

    def from_mix(g, back_mix):
        return select(dot(back_mix, r_ref[:, lanes_of(g)]))

    def from_affinity(g, affinity):
        high, low = split(dn_ref[:, lanes_of(g)])
        parts = []
        for p in range(2):
            pair = slice(p * 128, (p + 1) * 128)
            both = dot(
                affinity[p * 512 : (p + 1) * 512],
                jnp.concatenate([high[:, pair], low[:, pair]], axis=1),
            )
            both = both[:, :128] + both[:, 128:]
            parts.append(jnp.where(left, both[:C], both[C:]))
        return jnp.concatenate(parts, axis=1)

    def from_totals():
        high, low = split(dz_ref[...])
        return dot(vis, high) + dot(vis, low)

    def from_state(g):
        return carried * (
            dot_nt(part_of(qkvf_ref, 1, g), key_states[g])
            + dot_nt(part_of(qkvf_ref, 2, g), value_states[g])
            + norm_state[:, lanes_of(g)]
        )

    def to_slots(g, back_slots):
        written = jnp.exp(part_of(qkvf_ref, 3, g).astype(F32))
        d_ref[:, 3 * D + g * GROUP : 3 * D + (g + 1) * GROUP] = (back_slots * written).astype(BF16)

    norm = from_totals()
    mix = mixing(0)
    affinity = affine(0)
    mix_two = mixing(1)
    total = from_mix(0, mix)
    affinity_two = affine(1)
    total = total + from_affinity(0, affinity)
    total_two = from_mix(1, mix_two)
    to_slots(0, total + norm[:, lanes_of(0)] + from_state(0))
    total_two = total_two + from_affinity(1, affinity_two)
    to_slots(1, total_two + norm[:, lanes_of(1)] + from_state(1))


class Scatter:
    def __init__(self, count, source, own, axes, direct, out, buffers):
        self.axes, self.direct, self.out = axes, direct, out
        self.seq, self.at, self.sibling, self.beside = places()
        self.source, self.own = source, own
        self.core = lax.rem(self.seq, 2)
        self.total, self.local, self.last, self.done = buffers[:4]
        self.stages = []
        size = source.shape[0]
        base = 0
        for n, axis in enumerate(axes):
            ways = {"core": 2, "x": 2, "y": 2, "z": count // 2, "all": count}[axis]
            size = size // ways
            me = {
                "core": self.core, "x": self.seq // 2, "y": lax.rem(self.at, 2), "z": self.at // 2,
                "all": self.at,
            }[axis]
            held = source
            if own is not None and n > 0:
                held = own
            come, sems = buffers[4 + 2 * n], buffers[5 + 2 * n]
            self.stages.append((axis, ways, size, base, me, held, come, sems))
            if own is None or n > 0:
                base = base + me * size

    def copies(self, n):
        axis, ways, size, base, me, held, come, sems = self.stages[n]
        for k in range(1, ways):
            if axis in ("core", "x"):
                device = {"seq": self.sibling if axis == "core" else self.beside}
            else:
                device = {"fsdp": self.at ^ (2 * k if axis == "z" else k)}
            yield push(
                held.at[pl.ds(base + (me ^ k) * size, size)], come.at[k - 1],
                sems.at[0, k - 1], sems.at[1, k - 1], **device,
            )

    def copy_own(self):
        size = self.source.shape[0] // 2
        return pltpu.make_async_copy(
            self.source.at[pl.ds(self.core * size, size)], self.own, self.local
        )

    def start(self):
        for copy in self.copies(0):
            copy.start()
        if self.own is not None:
            self.copy_own().start()

    def advance(self, n):
        axis, ways, size, base, me, held, come, sems = self.stages[n]
        for copy in self.copies(n):
            copy.wait_recv()
        mine = held
        first = base + me * size
        if n == 0 and self.own is not None:
            self.copy_own().wait()
            mine, first = self.own, 0

        def added(slab):
            total = mine[first + slab].astype(F32)
            for k in range(1, ways):
                total = total + come[k - 1, slab].astype(F32)
            return total

        if n + 1 == len(self.stages):
            self.total[...] = added(0)
            self.copy_done().start()
            for copy in self.sent():
                copy.start()
            return

        @pl.loop(0, size)
        def _(slab):
            mine[first + slab] = added(slab).astype(mine.dtype)

        for copy in self.copies(n + 1):
            copy.start()

    def copy_done(self):
        return pltpu.make_async_copy(self.total, self.out.at[self.seq], self.done)

    def sent(self):
        other = lax.rem(self.sibling + 2, 4)
        for n, target in enumerate((self.sibling, self.beside, other)[: 3 if self.direct else 2]):
            yield push(
                self.total, self.out.at[self.seq], self.last.at[0, n], self.last.at[1, n], seq=target
            )

    def forwarded(self, source):
        here = self.out.at[source]
        return push(here, here, self.last.at[0, 2], self.last.at[1, 2], seq=self.sibling)

    def come_in(self, n, source):
        here = self.out.at[source]
        return push(here, here, self.last.at[0, n], self.last.at[1, n], seq=source)

    def forward(self):
        self.come_in(1, self.beside).wait_recv()
        self.forwarded(self.beside).start()

    def finish(self):
        other = lax.rem(self.sibling + 2, 4)
        self.come_in(0, self.sibling).wait_recv()
        if self.direct:
            self.come_in(1, self.beside).wait_recv()
        else:
            self.forwarded(self.beside).wait_send()
        self.forwarded(other).wait_recv()
        self.copy_done().wait()
        for copy in self.sent():
            copy.wait_send()
        for n in range(len(self.stages)):
            for copy in self.copies(n):
                copy.wait_send()


def scatter_scratch(count, part, lanes, link, axes, hbm):
    vmem, dma = pltpu.VMEM, pltpu.SemaphoreType.DMA
    size = 2 * 4 * count // 2
    out = [vmem((size // 2, part, lanes), link)] if hbm else []
    out += [vmem((part, lanes), F32), dma, dma((2, 3)), dma]
    for axis in axes:
        ways = {"core": 2, "x": 2, "y": 2, "z": count // 2, "all": count}[axis]
        size = size // ways
        out += [vmem((ways - 1, size, part, lanes), link), dma((2, ways - 1))]
    return out


OVER_X = ("core", "x", "y", "z")
OVER_Y = ("core", "y", "x", "z")
SHORT = ("core", "x", "all")


class SmallSum:
    def __init__(self, count, mine, from_seq, half, from_fsdp, sems):
        self.count, self.mine, self.from_seq = count, mine, from_seq
        self.half, self.from_fsdp, self.sems = half, from_fsdp, sems
        self.seq, self.at, _, _ = places()

    def lanes(self, owner):
        if self.from_fsdp.shape[2] == D:
            return pl.ds(0, D)
        first = owner * (D // self.count) // 128 * 128
        return pl.ds(pl.multiple_of(first, 128), 128)

    def over_seq(self, k, slot):
        return push(
            self.mine, self.from_seq.at[slot], self.sems[0].at[0, k], self.sems[0].at[1, k],
            seq=self.seq ^ k,
        )

    def over_fsdp(self, k):
        return push(
            self.half.at[:, self.lanes(self.at ^ k)], self.from_fsdp.at[self.at],
            self.sems[1].at[0, k], self.sems[1].at[1, k], fsdp=self.at ^ k,
        )

    def fsdp_in(self, k):
        here = self.from_fsdp.at[self.at ^ k]
        return push(here, here, self.sems[1].at[0, k], self.sems[1].at[1, k], fsdp=self.at ^ k)

    def start(self):
        for k in range(1, 4):
            self.over_seq(k, self.seq).start()
        self.from_seq[self.seq] = self.mine[...]

    def second(self):
        for k in range(1, 4):
            self.over_seq(k, self.seq ^ k).wait_recv()
        total = self.from_seq[0]
        for n in range(1, 4):
            total = total + self.from_seq[n]
        self.half[...] = total
        for k in range(1, self.count):
            self.over_fsdp(k).start()
        self.from_fsdp[self.at] = self.half[:, self.lanes(self.at)]

    def finish(self, out_ref):
        for k in range(1, self.count):
            self.fsdp_in(k).wait_recv()
        total = self.from_fsdp[0]
        for n in range(1, self.count):
            total = total + self.from_fsdp[n]
        out_ref[...] = total
        for k in range(1, 4):
            self.over_seq(k, self.seq).wait_send()
        for k in range(1, self.count):
            self.over_fsdp(k).wait_send()


def small_scratch(count, rows, lanes):
    vmem, dma = pltpu.VMEM, pltpu.SemaphoreType.DMA
    return [
        vmem((4, rows, D), F32), vmem((rows, D), F32), vmem((count, rows, lanes), F32),
        dma((2, 4)), dma((2, count)),
    ]


QUERY, COLUMN, SLOT, INPUT = 8, 16, 24, 32


def back_kernel(
    count, per, x_ref, xs_ref, qkvf_ref, do_ref, p_ref, s_ref, z_ref, kept_ref, dy_ref, doc_ref,
    small_ref, w_ref, ffg_ref, ffr_ref, ffs_ref,
    gi_ref, ff_out, fr_out, q_out, kv_out, f_out, s1_out, s2_out,
    gi_held, gi_sem, scores, scores_sem, d_all, h_turned, reading, numer, total, col_ref, edge_ref, head, state, heads, head_rows,
    snap, snap_rows, w_held, w_sem, q_piece, kv_piece, f_piece, last_small, *rest,
):
    step = pl.program_id(0)
    seq, at, _, _ = places()
    link = q_piece.dtype

    def take(size):
        nonlocal rest
        out, rest = rest[:size], rest[size:]
        return out

    (own,) = take(1)
    ff = Scatter(count, ffg_ref, own, OVER_X, False, ff_out, take(12))
    (own,) = take(1)
    fr = Scatter(count, ffr_ref, own, OVER_Y, False, fr_out, take(12))
    for_q = Scatter(count, q_piece, None, OVER_X, False, q_out, take(12))
    for_kv = Scatter(count, kv_piece, None, OVER_X, False, kv_out, take(12))
    for_f = Scatter(count, f_piece, None, SHORT, True, f_out, take(10))
    small_one = SmallSum(count, ffs_ref, *take(3), take(2))
    small_two = SmallSum(count, last_small, *take(3), take(2))
    states = States(heads, head_rows, take(2))

    def chunk(u, first, turned=False):
        n = step * per + u - first
        n = 7 - n if turned else n
        here = pl.ds(pl.multiple_of(n * C, C), C)
        block = pl.ds(pl.multiple_of((per - 1 - u if turned else u) * C, C), C)
        return n, here, block, col_ref[here], doc_ref[:, here].astype(F32)

    def fetch():
        return pltpu.make_async_copy(w_ref, w_held, w_sem)

    def fetch_scores(n):
        slot, here = lax.rem(n, 2), pl.ds(pl.multiple_of(n * per * C, per * C), per * C)
        return [
            pltpu.make_async_copy(ref.at[here], scores.at[slot, k], scores_sem.at[slot, k])
            for k, ref in enumerate((p_ref, s_ref, z_ref))
        ]

    def give(n):
        here = pl.ds(pl.multiple_of(n * per * C, per * C), per * C)
        slot = lax.rem(n, 2)
        return pltpu.make_async_copy(gi_held.at[slot], gi_ref.at[here], gi_sem.at[slot])

    def weight_grad(piece, d_lanes, lanes, short=False):
        grad = dot(h_turned[...], d_all[:, d_lanes])
        half, part = count // 2, piece.shape[1]
        for q in range(4):
            x, c = q // 2, q % 2
            share = grad[:, q * 128 : (q + 1) * 128].reshape(half, 2, part, 128).astype(link)
            if short:
                first = (c * 2 + x) * count
                piece[first : first + count, :, lanes] = share.reshape(count, part, 128)
                continue
            for y in range(2):
                first = ((c * 2 + x) * 2 + y) * half
                piece[first : first + half, :, lanes] = share[:, y]

    @pl.when(step == 0)
    def _():
        greet(count)
        for n in range(2):
            for copy in fetch_scores(n):
                copy.start()
        fetch().start()
        doc_parts(doc_ref, col_ref, edge_ref)
        head[...] = jnp.zeros_like(head)
        last_small[...] = jnp.zeros_like(last_small)

    def turn():
        weight_grad(q_piece, slice(0, D), slice(0, 128))
        for_q.start()
        states.finish()
        newest = edge_ref[15:16]
        state[...] = jnp.zeros_like(state)
        for n in range(4):
            use = jnp.where(head_rows[n, 1:2] == newest, 1.0, 0.0) * (n > seq).astype(F32)
            state[0:128] += use * heads[n].astype(F32)
            state[128:129] += use * head_rows[n, 0:1]

    def send_states():
        heads[seq] = head[0:128].astype(link)
        head_rows[seq, 0:1] = head[128:129]
        head_rows[seq, 1:2] = edge_ref[0:1]
        head_rows[seq, 2:8] = jnp.zeros((6, D), F32)
        states.start()

    def key_value_grads():
        weight_grad(kv_piece, slice(D, 2 * D), slice(0, 128))
        weight_grad(kv_piece, slice(2 * D, 3 * D), slice(128, 256))
        for_kv.start()

    def slot_grads():
        weight_grad(f_piece, slice(3 * D, 4 * D), slice(0, 128), True)
        for_f.start()

    def last():
        small_two.start()
        fr.forward()
        for_kv.forward()
        for_f.advance(2)
        small_two.second()
        for piece in (ff, fr, for_q):
            piece.finish()
        states.drain()
        small_two.finish(s2_out)
        for_kv.finish()
        for_f.finish()
        for n in (8 // per - 2, 8 // per - 1):
            give(n).wait()

    def begin():
        met(count)
        ff.start()
        small_one.start()

    schedule = {
        0: [begin],
        1: [fr.start],
        3: [lambda: ff.advance(0), small_one.second],
        5: [lambda: fr.advance(0)],
        QUERY - 1: [send_states],
        QUERY + 7: [turn],
        COLUMN: [lambda: ff.advance(1), lambda: fr.advance(1)],
        COLUMN + 1: [lambda: for_q.advance(0)],
        COLUMN + 5: [lambda: fr.advance(2)],
        COLUMN + 6: [lambda: ff.advance(2)],
        COLUMN + 7: [key_value_grads, lambda: for_q.advance(1)],
        SLOT + 1: [lambda: for_kv.advance(0), lambda: for_q.advance(2)],
        SLOT + 4: [lambda: ff.advance(3)],
        SLOT + 6: [lambda: for_kv.advance(1), lambda: fr.advance(3)],
        SLOT + 7: [slot_grads, lambda: for_q.advance(3)],
        INPUT + 1: [lambda: for_f.advance(0), lambda: for_kv.advance(2)],
        INPUT + 3: [ff.forward, for_q.forward, lambda: small_one.finish(s1_out)],
        INPUT + 5: [lambda: for_f.advance(1), lambda: for_kv.advance(3)],
        INPUT + 7: [last],
    }

    @pl.when(step < QUERY // per)
    def _():
        for copy in fetch_scores(step):
            copy.wait()

    @pl.loop(0, per)
    def _(u):
        at_chunk = step * per + u

        @pl.when(at_chunk < QUERY)
        def _():
            n, here, block, col, row = chunk(u, 0)
            kept_scores = [scores.at[lax.rem(step, 2), k, block] for k in range(3)]

            def aside():
                unit, _ = norm_parts(x_ref[block].astype(F32))
                h_turned[:, here] = (unit * small_ref[0:1] + small_ref[1:2]).astype(BF16).T

            row_body(
                n, qkvf_ref.at[block], do_ref.at[block], *kept_scores, kept_ref.at[pl.ds(u, 1)],
                col, row, edge_ref,
                reading.at[here], numer.at[here], total.at[here], head, aside,
            )

        @pl.when((at_chunk >= QUERY) & (at_chunk < COLUMN))
        def _():
            n, here, block, col, row = chunk(u, QUERY)
            query_body(
                n, qkvf_ref.at[block], kept_ref.at[pl.ds(u, 1)], col, row, edge_ref,
                numer.at[here], d_all.at[here, 0:D],
            )

        @pl.when((at_chunk >= COLUMN) & (at_chunk < SLOT))
        def _():
            n, here, block, col, row = chunk(u, COLUMN, True)
            column_body(
                n, qkvf_ref.at[block], do_ref.at[block], reading.at[here], numer.at[here],
                total.at[here], col, row, edge_ref, state, snap, snap_rows, d_all.at[here],
            )

        @pl.when((at_chunk >= SLOT) & (at_chunk < INPUT))
        def _():
            n, here, block, col, row = chunk(u, SLOT, True)
            slot_body(
                n, qkvf_ref.at[block], do_ref.at[block], reading.at[here], numer.at[here],
                total.at[here], col, row, edge_ref, snap, snap_rows, d_all.at[here],
            )

        @pl.when((at_chunk >= INPUT) & (u == 0))
        def _():
            nth = step - INPUT // per

            @pl.when(nth >= 2)
            def _():
                give(nth - 2).wait()

            @pl.when(nth == 0)
            def _():
                fetch().wait()

            size = xs_ref.shape[0]
            here = pl.ds(pl.multiple_of(nth * size, size), size)
            grad = dot_nt(d_all[here], w_held[...])
            unit, scale = norm_parts(xs_ref[...].astype(F32))
            last_small[0:1] += jnp.sum(grad * unit, axis=0, keepdims=True)
            last_small[1:2] += jnp.sum(grad, axis=0, keepdims=True)
            gi_held[lax.rem(nth, 2)] = dy_ref[...] + norm_back(unit, scale, small_ref[0:1], grad)
            give(nth).start()

        for when, actions in schedule.items():

            @pl.when(at_chunk == when)
            def _(actions=actions):
                for action in actions:
                    action()

    @pl.when(step + 2 < QUERY // per)
    def _():
        for copy in fetch_scores(step + 2):
            copy.start()


def back(
    count, tokens, qkvf, do, probs, score, inverse, kept, dy, doc_ids, small, w_all, ffg, ffr, ffs
):
    rows = tokens.shape[0]
    part, link = ffg.shape[1], ffg.dtype
    per = 2 if link == BF16 else 1
    size = per * C
    blocks = 8 // per
    once = lambda a: pl.BlockSpec(a.shape, lambda i: (0,) * a.ndim)
    anywhere = pl.BlockSpec(memory_space=pl.ANY)
    vmem, dma = pltpu.VMEM, pltpu.SemaphoreType.DMA

    def early(i):
        return jnp.minimum(i, blocks - 1)

    def twice(i):
        return jnp.where(i < blocks, i, jnp.clip(i - blocks, 0, blocks - 1))

    def turned(i):
        return blocks - 1 - lax.rem(jnp.clip(i - 2 * blocks, 0, 2 * blocks - 1), blocks)

    def always(i):
        return jnp.where(i < 2 * blocks, twice(i), turned(i))

    def both(i):
        return jnp.where(i < blocks, i, turned(i))

    late = lambda i: (jnp.maximum(i - 4 * blocks, 0), 0)
    tall = pl.BlockSpec((size, D), late)
    some = lambda lanes, order: pl.BlockSpec((size, lanes), lambda i: (order(i), 0))
    slabs = 4 * count
    return pl.pallas_call(
        functools.partial(back_kernel, count, per),
        grid=(5 * blocks,),
        in_specs=[some(D, early), tall, some(4 * D, always), some(D, both)]
        + [anywhere] * 3
        + [pl.BlockSpec((per, 128, D), lambda i: (twice(i), 0, 0)), tall]
        + [once(doc_ids), once(small), anywhere, anywhere, anywhere, once(ffs)],
        out_specs=[anywhere] * 6 + [whole(16, D), whole(8, 128)],
        out_shape=[
            shape_of((rows, D), F32),
            shape_of((4, part, 640), F32),
            shape_of((4, part, D), F32),
            shape_of((4, part, 128), F32),
            shape_of((4, part, 256), F32),
            shape_of((4, part, 128), F32),
            shape_of((16, D), F32),
            shape_of((8, 128), F32),
        ],
        scratch_shapes=[
            vmem((2, size, D), F32),
            dma((2,)),
            vmem((2, 3, size, D), F32),
            dma((2, 3)),
            vmem((rows, 4 * D), BF16),
            vmem((D, rows), BF16),
            vmem((rows, D), BF16),
            vmem((rows, D), F32),
            vmem((rows, D), F32),
            vmem((rows, 128), F32),
            vmem((16, D), F32),
            vmem((136, D), F32),
            vmem((136, D), F32),
            vmem((4, 128, D), link),
            vmem((4, 8, D), F32),
            vmem((8, 128, D), BF16),
            vmem((8, D), F32),
            vmem(w_all.shape, BF16),
            dma,
            vmem((slabs, part, 128), link),
            vmem((slabs, part, 256), link),
            vmem((slabs, part, 128), link),
            vmem((8, D), F32),
        ]
        + scatter_scratch(count, part, 640, link, OVER_X, True)
        + scatter_scratch(count, part, D, link, OVER_Y, True)
        + scatter_scratch(count, part, 128, link, OVER_X, False)
        + scatter_scratch(count, part, 256, link, OVER_X, False)
        + scatter_scratch(count, part, 128, link, SHORT, False)
        + small_scratch(count, 16, D)
        + small_scratch(count, 8, 128)
        + [dma((3, 2)), dma((3, 2))],
        compiler_params=pltpu.CompilerParams(
            vmem_limit_bytes=(62 if link == BF16 else 63) * MIB, collective_id=2, has_side_effects=True
        ),
        name="back",
    )(
        tokens, tokens, qkvf, do, probs, score, inverse, kept, dy, doc_ids, small, w_all, ffg, ffr,
        ffs,
    )


def finish_kernel(
    count, part, y_ref, gi_ref, ff_ref, fr_ref, q_ref, kv_ref, f_ref, s1_ref, s2_ref, y_out, gi_out,
    *rest,
):
    at = lax.axis_index("fsdp")
    *outs, held_y, held, sems = rest

    def move(n, out):
        source, through, target, here = gi_ref, held, gi_out, pl.ds(n * 512, 512)
        if n >= 4:
            source, through, target, here = y_ref, held_y, y_out, pl.ds((n - 4) * 1024, 1024)
        if out:
            return pltpu.make_async_copy(through.at[here], target.at[here], sems.at[1, n])
        return pltpu.make_async_copy(source.at[here], through.at[here], sems.at[0, n])

    def pick(row, size):
        out = row(0, size)
        for f in range(1, count):
            out = jnp.where(at == f, row(f * size, size), out)
        return out

    def bias(start, size):
        r = start // D
        return s1_ref[8 + r : 9 + r, start - r * D : start - r * D + size]

    def row_of_sums(ref, n):
        return lambda start, size: ref[
            n : n + 1, start % ref.shape[1] : start % ref.shape[1] + size
        ]

    for n in range(6):
        move(n, False).start()
    for n in range(4):
        lanes = slice(n * 128, (n + 1) * 128)
        outs[0][:, lanes] = q_ref[n]
        outs[1][:, lanes] = kv_ref[n, :, 0:128]
        outs[2][:, lanes] = kv_ref[n, :, 128:256]
        outs[3][:, lanes] = f_ref[n]
        outs[4][:, lanes] = ff_ref[n, :, 512:640]
        outs[5][:, n * 512 : (n + 1) * 512] = ff_ref[n, :, 0:512]
        for j in range(4):
            outs[6][j * part : (j + 1) * part, lanes] = fr_ref[n, :, j * 128 : (j + 1) * 128]
    for n in range(6):
        move(n, False).wait()
        move(n, True).start()
    outs[7][...] = pick(row_of_sums(s2_ref, 0), part)
    outs[8][...] = pick(row_of_sums(s2_ref, 1), part)
    outs[9][...] = pick(row_of_sums(s1_ref, 2), part)
    outs[10][...] = pick(row_of_sums(s1_ref, 3), part)
    outs[11][...] = pick(bias, 4 * part)
    outs[12][...] = pick(row_of_sums(s1_ref, 4), part)
    for n in range(6):
        move(n, True).wait()


def finish(count, part, out, grad_input, *sums):
    once = lambda shape: pl.BlockSpec(shape, lambda: (0,) * len(shape))
    anywhere = pl.BlockSpec(memory_space=pl.ANY)
    shapes = [(part, D)] * 5 + [(part, FF), (4 * part, D)]
    shapes += [(1, part)] * 4 + [(1, 4 * part), (1, part)]
    return pl.pallas_call(
        functools.partial(finish_kernel, count, part),
        in_specs=[anywhere] * 2 + [once(a.shape) for a in sums],
        out_specs=[anywhere] * 2 + [once(s) for s in shapes],
        out_shape=[shape_of(out.shape, BF16)]
        + [shape_of(s, F32) for s in (grad_input.shape, *shapes)],
        scratch_shapes=[
            pltpu.VMEM(out.shape, BF16),
            pltpu.VMEM(grad_input.shape, F32),
            pltpu.SemaphoreType.DMA((2, 6)),
        ],
        compiler_params=PARAMS,
        name="finish",
    )(out, grad_input, *sums)


def rows_of(lanes, order=lambda i: i):
    return pl.BlockSpec((C, lanes), lambda i: (order(i), 0))


def whole(*shape):
    return pl.BlockSpec(shape, lambda i: (0,) * len(shape))


def row_of(order=lambda i: i):
    return pl.BlockSpec((1, C), lambda i: (0, order(i)))


def shape_of(shape, kind):
    return jax.ShapeDtypeStruct(shape, kind)


PARAMS = pltpu.CompilerParams(vmem_limit_bytes=62 * MIB)


def on_device(
    tokens, doc_ids, w_query, w_key, w_value, w_slots, w_output, w_hidden, w_return,
    gain_first, shift_first, gain_second, shift_second, bias_hidden, bias_return, cotangent,
):
    rows = tokens.shape[0]
    count = lax.axis_size("fsdp")
    part = gain_first.shape[0]
    flat = lambda a: a.reshape(1, a.shape[0])
    found = front(
        count, tokens, doc_ids,
        (w_query, w_key, w_value, w_slots, w_output, w_hidden, w_return),
        [flat(a) for a in (gain_first, shift_first, gain_second, shift_second, bias_return)],
        flat(bias_hidden), cotangent,
    )
    grad_input, *sums = back(
        count, tokens, *(found[name] for name in ("qkvf_out", "do", "p", "s", "z", "kept", "dy")),
        doc_ids, found["vec"], found["w_out"].reshape(D, 4 * D).astype(BF16),
        found["pack"].reshape(-1, part, 640), found["pack_r"].reshape(-1, part, D), found["gsmall"],
    )
    out, grad_input, *grads = finish(count, part, found["y"], grad_input, *sums)
    return (out, grad_input, *grads[:7], *(a.reshape(-1) for a in grads[7:]))


def solution(mesh):
    tall, flat, one = P(("fsdp", "seq"), None), P("fsdp", None), P("fsdp")
    return jax.shard_map(
        on_device,
        mesh=mesh,
        in_specs=(tall, P("fsdp", "seq")) + (flat,) * 7 + (one,) * 6 + (tall,),
        out_specs=(tall, tall) + (flat,) * 7 + (one,) * 6,
        check_vma=False,
    )
```

profile of v0, /device:TPU:0, one launch (start us, length us, event | category | flops | bytes accessed | tf_op | source)
XLA Modules:
  0.0 198.5 jit_solution(10080423413122133251)
XLA Ops:
  0.7 103.1 %front.1 = (bf16[2048,2048]{1,0:T(8,128)(2,1)}, f32[2048,512]{1,0:T(8,128)}, f32[2048,512]{1,0:T(8,128)}, f32[2048,512]{1,0:T(8,128)}, f32[8,128,512]{2,1,0:T(8,...) custom-call(bf16[2048,512]{1,0:T(8,128)(2,1)} %xs_ref.1, ...), custom_call_target="tpu_custom_call" | custom-call | tf_op jit(solution)/shard_map/front/pallas_call | solution.py:901
  103.7 86.5 %back.1 = (f32[2048,512]{1,0:T(8,128)}, f32[4,64,640]{2,1,0:T(8,128)}, f32[4,64,512]{2,1,0:T(8,128)}, f32[4,64,128]{2,1,0:T(8,128)}, f32[4,64,256]{2,1,0:T(8,128...) custom-call(bf16[2048,512]{1,0:T(8,128)(2,1)} %xs_ref.1, bf16[2048,512]{1,0:T(8,128)(2,1)} %xs_ref.1, ...), custom_call_target="tpu_custom_call" | custom-call | tf_op jit(solution)/shard_map/back/pallas_call | solution.py:1613
  190.2 8.1 %finish.1 = (bf16[2048,512]{1,0:T(8,128)(2,1)}, f32[2048,512]{1,0:T(8,128)}, f32[64,512]{1,0:T(8,128)}, f32[64,512]{1,0:T(8,128)}, f32[64,512]{1,0:T(8,128)}, /*...) custom-call(bf16[2048,512]{1,0:T(8,128)(2,1)} %get-tuple-element.51., ...), custom_call_target="tpu_custom_call" | custom-call | tf_op jit(solution)/shard_map/finish/pallas_call | solution.py:1734
where the time goes:
time: 199 us; the launch traced here: 198 us
  Pallas kernels  198 us (99%)
    pallas_call x1, Pallas kernels, front(): pl.pallas_call(functools.partial(front_kernel, count, joined, (*ins, *out...  103 us
    pallas_call x1, Pallas kernels, back(): pl.pallas_call(functools.partial(back_kernel, count, per), grid=(5 * bloc...  86.5 us
    pallas_call x1, Pallas kernels, finish(): pl.pallas_call(functools.partial(finish_kernel, count, part), in_specs=[a...  8.09 us

commit v1 on v0

--- a/solution.py
+++ b/solution.py
@@ -162,8 +162,12 @@
     return ref[:, part * D + g * GROUP : part * D + (g + 1) * GROUP]
 
 
+def affinities(qkvf_ref, g, vis):
+    return masked(dot_nt(stacked(part_of(qkvf_ref, 0, g)), part_of(qkvf_ref, 1, g)), vis)
+
+
 def attend_body(
-    n, qkvf_ref, slots, vis, col, edge_ref, state, o_ref, p_ref, s_ref, z_ref, kept_ref
+    n, qkvf_ref, slots, vis, affine_ref, col, edge_ref, state, o_ref, p_ref, s_ref, z_ref, kept_ref
 ):
     kept_ref[0] = state[0:128]
     first = edge_ref[pl.ds(0, 1)]
@@ -176,9 +180,6 @@
     value_states = [expand(state[64:128, lanes_of(g)]).astype(BF16) for g in range(2)]
     norm_state = state[128:129]
 
-    def affine(g):
-        return masked(dot_nt(stacked(part_of(qkvf_ref, 0, g)), part_of(qkvf_ref, 1, g)), vis)
-
     def scores(g, affinity):
         lanes = lanes_of(g)
         numer = select(dot(affinity, slots[:, lanes]))
@@ -204,9 +205,8 @@
         out = select(dot(mix, part_of(qkvf_ref, 2, g))) + carried * dot(reading, value_states[g])
         o_ref[:, lanes_of(g)] = out.astype(BF16)
 
-    affinity = affine(0)
-    score, inverse = scores(0, affinity)
-    affinity = affine(1)
+    score, inverse = scores(0, affine_ref[...])
+    affinity = affinities(qkvf_ref, 1, vis)
     grown = grow(score)
     score_two, inverse_two = scores(1, affinity)
     reading = read(0, score, inverse, grown)
@@ -391,11 +391,13 @@
         for copy in self.hop(0, self.seq, self.sibling) + self.hop(1, self.seq, self.beside):
             copy.start()
 
-    def finish(self):
+    def forward(self):
         for copy in self.hop(1, self.beside, self.beside):
             copy.wait_recv()
         for copy in self.hop(2, self.beside, self.sibling):
             copy.start()
+
+    def finish(self):
         for copy in self.hop(0, self.sibling, self.sibling):
             copy.wait_recv()
         for copy in self.hop(2, lax.rem(self.sibling + 2, 4), self.sibling):
@@ -467,18 +469,20 @@
     return u * half, slope
 
 
+def feed_start(values, attended, vec_ref, w_out):
+    middle = values.astype(F32) + dot(attended, w_out())
+    unit, _ = norm_parts(middle)
+    return middle, (unit * vec_ref[2:3] + vec_ref[3:4]).astype(BF16)
+
+
 def feed_body(
-    values, attended, cot, vec_ref, bias_ref, w_out, w_hidden, w_return, ready,
+    middle, hidden, attended, cot, vec_ref, bias_ref, w_out, w_hidden, w_return,
     y_ref, dy_ref, do_ref, gsmall_ref, gwo_ref, gwh_ref, gwr_ref,
 ):
-    middle = values.astype(F32) + dot(attended, w_out())
-    unit, scale = norm_parts(middle)
-    hidden = (unit * vec_ref[2:3] + vec_ref[3:4]).astype(BF16)
     out = middle + vec_ref[4:5]
     grad_hidden = jnp.zeros_like(middle)
     cot32 = cot.astype(F32)
     tiles = FF // FEED_LANES
-    ready()
 
     def into(j):
         cols = slice(j * FEED_LANES, (j + 1) * FEED_LANES)
@@ -506,6 +510,8 @@
         to_out, to_hidden = outof(j, *bent)
         out = out + to_out
         grad_hidden = grad_hidden + to_hidden
+        if j == tiles // 2:
+            unit, scale = norm_parts(middle)
     y_ref[...] = out.astype(BF16)
     gsmall_ref[2:3] += jnp.sum(grad_hidden * unit, axis=0, keepdims=True)
     gsmall_ref[3:4] += jnp.sum(grad_hidden, axis=0, keepdims=True)
@@ -527,7 +533,7 @@
         for y in range(2):
             over_x, over_y = ((c * 2 + x) * 2 + y) * half, ((c * 2 + y) * 2 + x) * half
             put(0, over_x, slice(0, 512), hidden_part[:, y])
-            put(0, over_x, slice(512, 640), out_part[:, y])
+            put(1, over_y, slice(512, 640), out_part[:, y])
             for j in range(4):
                 put(1, over_y, slice(j * 128, (j + 1) * 128), turned[:, y, j])
 
@@ -544,9 +550,10 @@
         for ref in (gwo_ref, gwh_ref, gwr_ref, gsmall_ref):
             ref[...] = jnp.zeros_like(ref)
 
+    views = weight_views(wo_ref, wh_ref, wr_ref)
     feed_body(
-        x_ref[...], o_ref[...], g_ref[...], small_ref, bias_ref, *weight_views(wo_ref, wh_ref, wr_ref),
-        lambda: None, y_ref, dy_ref, do_ref, gsmall_ref, gwo_ref, gwh_ref, gwr_ref,
+        *feed_start(x_ref[...], o_ref[...], small_ref, views[0]), o_ref[...], g_ref[...], small_ref,
+        bias_ref, *views, y_ref, dy_ref, do_ref, gsmall_ref, gwo_ref, gwh_ref, gwr_ref,
     )
 
     @pl.when(step == pl.num_programs(0) - 1)
@@ -582,6 +589,7 @@
     mine_o, mine_h, mine_r, spread, smalls = r.mine_o, r.mine_h, r.mine_r, r.spread, r.smalls
     col_ref, edge_ref, state, tail = r.col, r.edge, r.state, r.tail
     tails, tail_rows = r.tails, r.tail_rows
+    slots = r.o if joined else r.slots
     step = pl.program_id(0)
     seq, at, _, _ = places()
     link = mine.dtype
@@ -639,8 +647,8 @@
                 hidden[here] = (unit * vec_out[0:1] + vec_out[1:2]).astype(BF16)
 
         main.at_once(between)
+        q_piece.second()
         h_piece.start()
-        r_piece.start()
 
     @pl.when(step < FRONT)
     def _():
@@ -658,8 +666,12 @@
 
     @pl.when(step == 1)
     def _():
-        q_piece.second()
         o_piece.second()
+        r_piece.start()
+
+    @pl.when(step == FRONT - 2)
+    def _():
+        q_piece.third()
 
     @pl.when(step == FRONT - 1)
     def _():
@@ -668,8 +680,15 @@
         tail_rows[seq, 1:2] = edge_ref[15:16]
         tail_rows[seq, 2:8] = jnp.zeros((6, D), F32)
         states.start()
-        q_piece.third()
+
+        @pl.loop(0, 8)
+        def _(n):
+            here = pl.ds(pl.multiple_of(n * C, C), C)
+            slots[here] = jnp.exp(qkvf[here, 3 * D :].astype(F32)).astype(BF16)
+            r.seen[n] = visible(col_ref[here], doc_ref[:, here].astype(F32))
+
         q_piece.finish()
+        h_piece.second()
 
         @pl.loop(0, FRONT)
         def _(n):
@@ -684,10 +703,10 @@
 
         @pl.loop(0, 8)
         def _(n):
-            here = pl.ds(pl.multiple_of(n * C, C), C)
-            hidden[here] = jnp.exp(qkvf[here, 3 * D :].astype(F32)).astype(BF16)
-            r.seen[n] = visible(col_ref[here], doc_ref[:, here].astype(F32))
-
+            rows = qkvf.at[pl.ds(pl.multiple_of(n * C, C), C)]
+            r.affine[n] = affinities(rows, 0, r.seen[n])
+
+        states.forward()
         states.finish()
         first = edge_ref[0:1]
         state[...] = jnp.zeros_like(state)
@@ -695,37 +714,39 @@
             use = jnp.where(tail_rows[n, 1:2] == first, 1.0, 0.0) * (n < seq).astype(F32)
             state[0:128] += use * tails[n].astype(F32)
             state[128:129] += use * tail_rows[n, 0:1]
-        h_piece.second()
+        h_piece.third()
 
     per = 8 // FRONT
 
     def kept_copies(n):
-        here = pl.ds(pl.multiple_of(n * per * C, per * C), per * C)
+        here = pl.ds(pl.multiple_of(n * C, C), C)
         slot = lax.rem(n, 2)
         return [
             pltpu.make_async_copy(r.stage.at[slot, k], out.at[here], stage_sem.at[slot, k])
             for k, out in enumerate((r.p, r.s, r.z))
         ]
 
-    @pl.when((step >= FRONT + 2) & (step < 2 * FRONT))
-    def _():
-        for copy in kept_copies(step - FRONT - 2):
-            copy.wait()
-
     @pl.when((step >= FRONT) & (step < 2 * FRONT))
     def _():
-        slot = lax.rem(step - FRONT, 2)
-
-        @pl.loop(0, per)
+        @pl.loop(0, per, unroll=True)
         def _(u):
             n = (step - FRONT) * per + u
+            slot = lax.rem(n, 2)
+
+            @pl.when(n >= 2)
+            def _():
+                for copy in kept_copies(n - 2):
+                    copy.wait()
+
             here = pl.ds(pl.multiple_of(n * C, C), C)
             block = pl.ds(pl.multiple_of(u * C, C), C)
             attend_body(
-                n, qkvf.at[here], hidden[here], r.seen[n], col_ref[here], edge_ref, state,
-                r.o.at[here if joined else block], *(r.stage.at[slot, k, block] for k in range(3)),
+                n, qkvf.at[here], slots[here], r.seen[n], r.affine.at[n], col_ref[here], edge_ref, state,
+                r.o.at[here if joined else block], *(r.stage.at[slot, k] for k in range(3)),
                 r.kept.at[pl.ds(u, 1)],
             )
+            for copy in kept_copies(n):
+                copy.start()
 
             @pl.when(n == 0)
             def _():
@@ -735,19 +756,13 @@
             def _():
                 r_piece.second()
 
-            @pl.when(n == per)
+            @pl.when(n == 6)
             def _():
-                h_piece.third()
-
-    @pl.when((step >= FRONT) & (step < 2 * FRONT))
-    def _():
-        for copy in kept_copies(step - FRONT):
-            copy.start()
+                h_piece.fourth()
 
     @pl.when(step == 2 * FRONT - 1)
     def _():
         r_piece.third()
-        h_piece.fourth()
         o_piece.finish()
         for copy in save():
             copy.wait()
@@ -761,7 +776,7 @@
         states.drain()
         for k in range(1, count):
             small_copy(k, at).wait_send()
-        for n in (FRONT - 2, FRONT - 1):
+        for n in (6, 7):
             for copy in kept_copies(n):
                 copy.wait()
 
@@ -769,10 +784,19 @@
         pl.when(step == 2 * FRONT - 1)(complete)
         return
 
-    @pl.when(step == 2 * FRONT)
+    views = weight_views(r.wo_all, r.wh_all, r.wr_all)
+
+    @pl.when(step == 2 * FRONT - 1)
     def _():
         for ref in (r.gwo, r.gwh, r.gwr, r.gsmall):
             ref[...] = jnp.zeros_like(ref)
+
+        @pl.loop(0, x_ref.shape[0] // FEED_ROWS)
+        def _(n):
+            here = pl.ds(pl.multiple_of(n * FEED_ROWS, FEED_ROWS), FEED_ROWS)
+            r.middle[here], hidden[here] = feed_start(x_ref[here], r.o[here], vec_out, views[0])
+
+        complete()
 
     fed = step - 2 * FRONT
 
@@ -795,9 +819,7 @@
         here = pl.ds(pl.multiple_of(fed * FEED_ROWS, FEED_ROWS), FEED_ROWS)
         slot = lax.rem(fed, 2)
         feed_body(
-            x_ref[here], r.o[here], r.g[...], vec_out, bias_out,
-            *weight_views(r.wo_all, r.wh_all, r.wr_all),
-            lambda: pl.when(step == 2 * FRONT)(complete),
+            r.middle[here], hidden[here], r.o[here], r.g[...], vec_out, bias_out, *views,
             r.held_y.at[slot], r.held_dy.at[slot], r.held_do.at[slot], r.gsmall, r.gwo, r.gwh, r.gwr,
         )
         for copy in fed_copies(fed):
@@ -809,15 +831,15 @@
 
         def put(which, slab, lanes, values):
             n = values.shape[0] * part
-            at_lane = 640 * which + lanes.start
+            at_lane = D * which + lanes.start
             qkvf[slab * part : slab * part + n, at_lane : at_lane + values.shape[2]] = (
                 values.reshape(n, -1).astype(BF16)
             )
 
         pack_grads(count, part, r.gwo, r.gwh, r.gwr, put)
         copies = [
-            pltpu.make_async_copy(qkvf.at[:, 0:640], r.pack, out_sem.at[0]),
-            pltpu.make_async_copy(qkvf.at[:, 640:1152], r.pack_r, out_sem.at[1]),
+            pltpu.make_async_copy(qkvf.at[:, 0:D], r.pack, out_sem.at[0]),
+            pltpu.make_async_copy(qkvf.at[:, D:1152], r.pack_r, out_sem.at[1]),
         ]
         for copy in copies:
             copy.start()
@@ -870,8 +892,9 @@
         "tail": vmem((136, D), F32),
         "tails": vmem((4, 128, D), link),
         "tail_rows": vmem((4, 8, D), F32),
-        "stage": vmem((2, 3, per * C, D), F32),
+        "stage": vmem((2, 3, C, D), F32),
         "seen": vmem((8, C, C), BF16),
+        "affine": vmem((8, 4 * C, C), BF16),
     }
     gathered = {
         "wo_all": (count, part, D), "wh_all": (count, part, FF), "wr_all": (count, 4 * part, D),
@@ -882,14 +905,15 @@
             "y": (shape_of((rows, D), BF16), anywhere),
             "dy": (wide_rows, anywhere),
             "do": (shape_of((rows, D), BF16), anywhere),
-            "pack": (shape_of((slabs * part, 640), BF16), anywhere),
-            "pack_r": (shape_of((slabs * part, D), BF16), anywhere),
+            "pack": (shape_of((slabs * part, D), BF16), anywhere),
+            "pack_r": (shape_of((slabs * part, 640), BF16), anywhere),
             "gsmall": (shape_of((16, D), F32), whole(16, D)),
         }
         scratch |= {name: vmem(shape, link) for name, shape in gathered.items()}
         scratch |= {
             "held_y": vmem((2, FEED_ROWS, D), BF16), "held_dy": vmem((2, FEED_ROWS, D), F32),
             "held_do": vmem((2, FEED_ROWS, D), BF16),
+            "middle": vmem((rows, D), F32),
             "o": vmem((rows, D), BF16), "bias": vmem((1, FF), F32), "gwo": vmem((D, D), F32),
             "gwh": vmem((D, FF), F32), "gwr": vmem((D, FF), F32),
         }
@@ -898,6 +922,7 @@
         outs |= {
             "o": (shape_of((rows, D), BF16), tall), "bias": (shape_of((1, FF), F32), whole(1, FF)),
         }
+        scratch["slots"] = vmem((rows, D), BF16)
     found = pl.pallas_call(
         functools.partial(front_kernel, count, joined, (*ins, *outs, *scratch)),
         grid=(2 * FRONT + (rows // FEED_ROWS if joined else 0),),
@@ -934,13 +959,13 @@
                 + [whole(8, D), whole(1, FF)]
                 + [whole(*a.shape) for a in weights],
                 out_specs=[tall] * 3
-                + [whole(slabs * part, 640), whole(slabs * part, D), whole(16, D)],
+                + [whole(slabs * part, D), whole(slabs * part, 640), whole(16, D)],
                 out_shape=[
                     shape_of((rows, D), BF16),
                     shape_of((rows, D), F32),
                     shape_of((rows, D), BF16),
+                    shape_of((slabs * part, D), link),
                     shape_of((slabs * part, 640), link),
-                    shape_of((slabs * part, D), link),
                     shape_of((16, D), F32),
                 ],
                 scratch_shapes=[
@@ -1177,11 +1202,20 @@
             if own is None or n > 0:
                 base = base + me * size
 
-    def copies(self, n):
+    def copies(self, n, halves=(0, 1)):
         axis, ways, size, base, me, held, come, sems = self.stages[n]
+        if axis == "x":
+            for half in halves:
+                first, some = half * (size // 2), size // 2
+                yield push(
+                    held.at[pl.ds(base + (me ^ 1) * size + first, some)],
+                    come.at[0, pl.ds(first, some)],
+                    sems.at[0, half], sems.at[1, half], seq=self.beside,
+                )
+            return
         for k in range(1, ways):
-            if axis in ("core", "x"):
-                device = {"seq": self.sibling if axis == "core" else self.beside}
+            if axis == "core":
+                device = {"seq": self.sibling}
             else:
                 device = {"fsdp": self.at ^ (2 * k if axis == "z" else k)}
             yield push(
@@ -1201,7 +1235,7 @@
         if self.own is not None:
             self.copy_own().start()
 
-    def advance(self, n):
+    def advance(self, n, halves=(0, 1)):
         axis, ways, size, base, me, held, come, sems = self.stages[n]
         for copy in self.copies(n):
             copy.wait_recv()
@@ -1228,7 +1262,7 @@
         def _(slab):
             mine[first + slab] = added(slab).astype(mine.dtype)
 
-        for copy in self.copies(n + 1):
+        for copy in self.copies(n + 1, halves):
             copy.start()
 
     def copy_done(self):
@@ -1277,7 +1311,7 @@
     for axis in axes:
         ways = {"core": 2, "x": 2, "y": 2, "z": count // 2, "all": count}[axis]
         size = size // ways
-        out += [vmem((ways - 1, size, part, lanes), link), dma((2, ways - 1))]
+        out += [vmem((ways - 1, size, part, lanes), link), dma((2, max(ways - 1, 2)))]
     return out
 
 
@@ -1457,8 +1491,8 @@
 
     def last():
         small_two.start()
-        fr.forward()
-        for_kv.forward()
+        for piece in (fr, ff, for_q, for_kv):
+            piece.forward()
         for_f.advance(2)
         small_two.second()
         for piece in (ff, fr, for_q):
@@ -1470,6 +1504,10 @@
         for n in (8 // per - 2, 8 // per - 1):
             give(n).wait()
 
+    def rest_of_ff():
+        for copy in ff.copies(1, (1,)):
+            copy.start()
+
     def begin():
         met(count)
         ff.start()
@@ -1478,21 +1516,21 @@
     schedule = {
         0: [begin],
         1: [fr.start],
-        3: [lambda: ff.advance(0), small_one.second],
+        3: [lambda: ff.advance(0, (0,)), small_one.second],
         5: [lambda: fr.advance(0)],
         QUERY - 1: [send_states],
+        QUERY + 5: [states.forward, rest_of_ff],
         QUERY + 7: [turn],
-        COLUMN: [lambda: ff.advance(1), lambda: fr.advance(1)],
-        COLUMN + 1: [lambda: for_q.advance(0)],
-        COLUMN + 5: [lambda: fr.advance(2)],
-        COLUMN + 6: [lambda: ff.advance(2)],
+        COLUMN + 1: [lambda: fr.advance(1), lambda: for_q.advance(0)],
+        COLUMN + 2: [lambda: ff.advance(1)],
+        COLUMN + 6: [lambda: fr.advance(2)],
+        SLOT: [lambda: ff.advance(2)],
         COLUMN + 7: [key_value_grads, lambda: for_q.advance(1)],
         SLOT + 1: [lambda: for_kv.advance(0), lambda: for_q.advance(2)],
-        SLOT + 4: [lambda: ff.advance(3)],
         SLOT + 6: [lambda: for_kv.advance(1), lambda: fr.advance(3)],
-        SLOT + 7: [slot_grads, lambda: for_q.advance(3)],
+        SLOT + 7: [slot_grads, lambda: ff.advance(3), lambda: for_q.advance(3)],
         INPUT + 1: [lambda: for_f.advance(0), lambda: for_kv.advance(2)],
-        INPUT + 3: [ff.forward, for_q.forward, lambda: small_one.finish(s1_out)],
+        INPUT + 3: [lambda: small_one.finish(s1_out)],
         INPUT + 5: [lambda: for_f.advance(1), lambda: for_kv.advance(3)],
         INPUT + 7: [last],
     }
@@ -1620,8 +1658,8 @@
         out_specs=[anywhere] * 6 + [whole(16, D), whole(8, 128)],
         out_shape=[
             shape_of((rows, D), F32),
+            shape_of((4, part, D), F32),
             shape_of((4, part, 640), F32),
-            shape_of((4, part, D), F32),
             shape_of((4, part, 128), F32),
             shape_of((4, part, 256), F32),
             shape_of((4, part, 128), F32),
@@ -1653,8 +1691,8 @@
             vmem((slabs, part, 128), link),
             vmem((8, D), F32),
         ]
-        + scatter_scratch(count, part, 640, link, OVER_X, True)
-        + scatter_scratch(count, part, D, link, OVER_Y, True)
+        + scatter_scratch(count, part, D, link, OVER_X, True)
+        + scatter_scratch(count, part, 640, link, OVER_Y, True)
         + scatter_scratch(count, part, 128, link, OVER_X, False)
         + scatter_scratch(count, part, 256, link, OVER_X, False)
         + scatter_scratch(count, part, 128, link, SHORT, False)
@@ -1709,8 +1747,8 @@
         outs[1][:, lanes] = kv_ref[n, :, 0:128]
         outs[2][:, lanes] = kv_ref[n, :, 128:256]
         outs[3][:, lanes] = f_ref[n]
-        outs[4][:, lanes] = ff_ref[n, :, 512:640]
-        outs[5][:, n * 512 : (n + 1) * 512] = ff_ref[n, :, 0:512]
+        outs[4][:, lanes] = fr_ref[n, :, 512:640]
+        outs[5][:, n * 512 : (n + 1) * 512] = ff_ref[n]
         for j in range(4):
             outs[6][j * part : (j + 1) * part, lanes] = fr_ref[n, :, j * 128 : (j + 1) * 128]
     for n in range(6):
@@ -1783,7 +1821,7 @@
     grad_input, *sums = back(
         count, tokens, *(found[name] for name in ("qkvf_out", "do", "p", "s", "z", "kept", "dy")),
         doc_ids, found["vec"], found["w_out"].reshape(D, 4 * D).astype(BF16),
-        found["pack"].reshape(-1, part, 640), found["pack_r"].reshape(-1, part, D), found["gsmall"],
+        found["pack"].reshape(-1, part, D), found["pack_r"].reshape(-1, part, 640), found["gsmall"],
     )
     out, grad_input, *grads = finish(count, part, found["y"], grad_input, *sums)
     return (out, grad_input, *grads[:7], *(a.reshape(-1) for a in grads[7:]))

time: 199 us -> 195 us (0.980)
  Pallas kernels: 198 us -> 194 us
    pallas_call x1, Pallas kernels: 103 us -> 98.7 us  [front(): pl.pallas_call(functools.partial(front_kernel, count, joined, (*ins, *out...]
where the time goes in v1:
time: 195 us; the launch traced here: 194 us
  Pallas kernels  194 us (99%)
    pallas_call x1, Pallas kernels, front(): pl.pallas_call(functools.partial(front_kernel, count, joined, (*ins, *out...  98.7 us
    pallas_call x1, Pallas kernels, back(): pl.pallas_call(functools.partial(back_kernel, count, per), grid=(5 * bloc...  86.8 us
    pallas_call x1, Pallas kernels, finish(): pl.pallas_call(functools.partial(finish_kernel, count, part), in_specs=[a...  8.09 us

profile of v1, /device:TPU:0, one launch (start us, length us, event | category | flops | bytes accessed | tf_op | source)
XLA Modules:
  0.0 194.4 jit_solution(16764566514655999466)
XLA Ops:
  0.7 98.7 %front.1 = (bf16[2048,2048]{1,0:T(8,128)(2,1)}, f32[2048,512]{1,0:T(8,128)}, f32[2048,512]{1,0:T(8,128)}, f32[2048,512]{1,0:T(8,128)}, f32[8,128,512]{2,1,0:T(8,...) custom-call(bf16[2048,512]{1,0:T(8,128)(2,1)} %xs_ref.1, ...), custom_call_target="tpu_custom_call" | custom-call | tf_op jit(solution)/shard_map/front/pallas_call | solution.py:926
  99.4 86.8 %back.1 = (f32[2048,512]{1,0:T(8,128)}, f32[4,64,512]{2,1,0:T(8,128)}, f32[4,64,640]{2,1,0:T(8,128)}, f32[4,64,128]{2,1,0:T(8,128)}, f32[4,64,256]{2,1,0:T(8,128...) custom-call(bf16[2048,512]{1,0:T(8,128)(2,1)} %xs_ref.1, bf16[2048,512]{1,0:T(8,128)(2,1)} %xs_ref.1, ...), custom_call_target="tpu_custom_call" | custom-call | tf_op jit(solution)/shard_map/back/pallas_call | solution.py:1651
  186.2 8.1 %finish.1 = (bf16[2048,512]{1,0:T(8,128)(2,1)}, f32[2048,512]{1,0:T(8,128)}, f32[64,512]{1,0:T(8,128)}, f32[64,512]{1,0:T(8,128)}, f32[64,512]{1,0:T(8,128)}, /*...) custom-call(bf16[2048,512]{1,0:T(8,128)(2,1)} %get-tuple-element.51., ...), custom_call_target="tpu_custom_call" | custom-call | tf_op jit(solution)/shard_map/finish/pallas_call | solution.py:1772

commit v2 on v1

--- a/solution.py
+++ b/solution.py
@@ -645,6 +645,11 @@
                 here = pl.ds(pl.multiple_of(n * C, C), C)
                 unit, _ = norm_parts(x_ref[here].astype(F32))
                 hidden[here] = (unit * vec_out[0:1] + vec_out[1:2]).astype(BF16)
+                r.seen[n] = visible(col_ref[here], doc_ref[:, here].astype(F32))
+
+            if joined:
+                for ref in (r.gwo, r.gwh, r.gwr, r.gsmall):
+                    ref[...] = jnp.zeros_like(ref)
 
         main.at_once(between)
         q_piece.second()
@@ -685,7 +690,6 @@
         def _(n):
             here = pl.ds(pl.multiple_of(n * C, C), C)
             slots[here] = jnp.exp(qkvf[here, 3 * D :].astype(F32)).astype(BF16)
-            r.seen[n] = visible(col_ref[here], doc_ref[:, here].astype(F32))
 
         q_piece.finish()
         h_piece.second()
@@ -788,9 +792,6 @@
 
     @pl.when(step == 2 * FRONT - 1)
     def _():
-        for ref in (r.gwo, r.gwh, r.gwr, r.gsmall):
-            ref[...] = jnp.zeros_like(ref)
-
         @pl.loop(0, x_ref.shape[0] // FEED_ROWS)
         def _(n):
             here = pl.ds(pl.multiple_of(n * FEED_ROWS, FEED_ROWS), FEED_ROWS)
@@ -1491,10 +1492,12 @@
 
     def last():
         small_two.start()
-        for piece in (fr, ff, for_q, for_kv):
+        small_one.finish(s1_out)
+        for piece in (ff, for_q):
             piece.forward()
+        small_two.second()
         for_f.advance(2)
-        small_two.second()
+        for_kv.forward()
         for piece in (ff, fr, for_q):
             piece.finish()
         states.drain()
@@ -1528,9 +1531,9 @@
         COLUMN + 7: [key_value_grads, lambda: for_q.advance(1)],
         SLOT + 1: [lambda: for_kv.advance(0), lambda: for_q.advance(2)],
         SLOT + 6: [lambda: for_kv.advance(1), lambda: fr.advance(3)],
-        SLOT + 7: [slot_grads, lambda: ff.advance(3), lambda: for_q.advance(3)],
+        SLOT + 7: [slot_grads],
         INPUT + 1: [lambda: for_f.advance(0), lambda: for_kv.advance(2)],
-        INPUT + 3: [lambda: small_one.finish(s1_out)],
+        INPUT + 3: [lambda: ff.advance(3), lambda: for_q.advance(3), fr.forward],
         INPUT + 5: [lambda: for_f.advance(1), lambda: for_kv.advance(3)],
         INPUT + 7: [last],
     }
@@ -1709,12 +1712,13 @@
     )
 
 
-def finish_kernel(
-    count, part, y_ref, gi_ref, ff_ref, fr_ref, q_ref, kv_ref, f_ref, s1_ref, s2_ref, y_out, gi_out,
-    *rest,
-):
+def finish_kernel(count, part, *refs):
     at = lax.axis_index("fsdp")
-    *outs, held_y, held, sems = rest
+    y_ref, gi_ref, *sums = refs[:7]
+    s1_ref, s2_ref, y_out, gi_out, *rest = refs[7:]
+    outs, (held_y, held, *rest) = rest[:13], rest[13:]
+    ff_ref, fr_ref, q_ref, kv_ref, f_ref = rest[:5]
+    staged, sems, sum_sems = rest[5:12], rest[12], rest[13]
 
     def move(n, out):
         source, through, target, here = gi_ref, held, gi_out, pl.ds(n * 512, 512)
@@ -1724,6 +1728,12 @@
             return pltpu.make_async_copy(through.at[here], target.at[here], sems.at[1, n])
         return pltpu.make_async_copy(source.at[here], through.at[here], sems.at[0, n])
 
+    def bring(n):
+        return pltpu.make_async_copy(sums[n], rest[n], sum_sems.at[0, n])
+
+    def give(n):
+        return pltpu.make_async_copy(staged[n], outs[n], sum_sems.at[1, n])
+
     def pick(row, size):
         out = row(0, size)
         for f in range(1, count):
@@ -1739,18 +1749,24 @@
             n : n + 1, start % ref.shape[1] : start % ref.shape[1] + size
         ]
 
+    for n in range(5):
+        bring(n).start()
     for n in range(6):
         move(n, False).start()
+    for n in range(5):
+        bring(n).wait()
     for n in range(4):
         lanes = slice(n * 128, (n + 1) * 128)
-        outs[0][:, lanes] = q_ref[n]
-        outs[1][:, lanes] = kv_ref[n, :, 0:128]
-        outs[2][:, lanes] = kv_ref[n, :, 128:256]
-        outs[3][:, lanes] = f_ref[n]
-        outs[4][:, lanes] = fr_ref[n, :, 512:640]
-        outs[5][:, n * 512 : (n + 1) * 512] = ff_ref[n]
+        staged[0][:, lanes] = q_ref[n]
+        staged[1][:, lanes] = kv_ref[n, :, 0:128]
+        staged[2][:, lanes] = kv_ref[n, :, 128:256]
+        staged[3][:, lanes] = f_ref[n]
+        staged[4][:, lanes] = fr_ref[n, :, 512:640]
+        staged[5][:, n * 512 : (n + 1) * 512] = ff_ref[n]
         for j in range(4):
-            outs[6][j * part : (j + 1) * part, lanes] = fr_ref[n, :, j * 128 : (j + 1) * 128]
+            staged[6][j * part : (j + 1) * part, lanes] = fr_ref[n, :, j * 128 : (j + 1) * 128]
+    for n in range(7):
+        give(n).start()
     for n in range(6):
         move(n, False).wait()
         move(n, True).start()
@@ -1760,6 +1776,8 @@
     outs[10][...] = pick(row_of_sums(s1_ref, 3), part)
     outs[11][...] = pick(bias, 4 * part)
     outs[12][...] = pick(row_of_sums(s1_ref, 4), part)
+    for n in range(7):
+        give(n).wait()
     for n in range(6):
         move(n, True).wait()
 
@@ -1767,19 +1785,19 @@
 def finish(count, part, out, grad_input, *sums):
     once = lambda shape: pl.BlockSpec(shape, lambda: (0,) * len(shape))
     anywhere = pl.BlockSpec(memory_space=pl.ANY)
-    shapes = [(part, D)] * 5 + [(part, FF), (4 * part, D)]
-    shapes += [(1, part)] * 4 + [(1, 4 * part), (1, part)]
+    vmem, dma = pltpu.VMEM, pltpu.SemaphoreType.DMA
+    large = [(part, D)] * 5 + [(part, FF), (4 * part, D)]
+    small = [(1, part)] * 4 + [(1, 4 * part), (1, part)]
     return pl.pallas_call(
         functools.partial(finish_kernel, count, part),
-        in_specs=[anywhere] * 2 + [once(a.shape) for a in sums],
-        out_specs=[anywhere] * 2 + [once(s) for s in shapes],
+        in_specs=[anywhere] * 7 + [once(a.shape) for a in sums[5:]],
+        out_specs=[anywhere] * 9 + [once(s) for s in small],
         out_shape=[shape_of(out.shape, BF16)]
-        + [shape_of(s, F32) for s in (grad_input.shape, *shapes)],
-        scratch_shapes=[
-            pltpu.VMEM(out.shape, BF16),
-            pltpu.VMEM(grad_input.shape, F32),
-            pltpu.SemaphoreType.DMA((2, 6)),
-        ],
+        + [shape_of(s, F32) for s in (grad_input.shape, *large, *small)],
+        scratch_shapes=[vmem(out.shape, BF16), vmem(grad_input.shape, F32)]
+        + [vmem(a.shape, F32) for a in sums[:5]]
+        + [vmem(s, F32) for s in large]
+        + [dma((2, 6)), dma((2, 7))],
         compiler_params=PARAMS,
         name="finish",
     )(out, grad_input, *sums)

time: 195 us -> 192 us (0.985)
  Pallas kernels: 194 us -> 191 us
where the time goes in v2:
time: 192 us
  Pallas kernels  191 us (99%)
    pallas_call x1, Pallas kernels, front(): pl.pallas_call(functools.partial(front_kernel, count, joined, (*ins, *out...  98.2 us
    pallas_call x1, Pallas kernels, back(): pl.pallas_call(functools.partial(back_kernel, count, per), grid=(5 * bloc...  85.2 us
    pallas_call x1, Pallas kernels, finish(): pl.pallas_call(functools.partial(finish_kernel, count, part), in_specs=[a...  7.71 us

profile of v2, /device:TPU:0, one launch (start us, length us, event | category | flops | bytes accessed | tf_op | source)
XLA Modules:
  0.0 192.0 jit_solution(15361458177898169545)
XLA Ops:
  0.7 98.2 %front.1 = (bf16[2048,2048]{1,0:T(8,128)(2,1)}, f32[2048,512]{1,0:T(8,128)}, f32[2048,512]{1,0:T(8,128)}, f32[2048,512]{1,0:T(8,128)}, f32[8,128,512]{2,1,0:T(8,...) custom-call(bf16[2048,512]{1,0:T(8,128)(2,1)} %xs_ref.1, ...), custom_call_target="tpu_custom_call" | custom-call | tf_op jit(solution)/shard_map/front/pallas_call | solution.py:927
  98.9 85.2 %back.1 = (f32[2048,512]{1,0:T(8,128)}, f32[4,64,512]{2,1,0:T(8,128)}, f32[4,64,640]{2,1,0:T(8,128)}, f32[4,64,128]{2,1,0:T(8,128)}, f32[4,64,256]{2,1,0:T(8,128...) custom-call(bf16[2048,512]{1,0:T(8,128)(2,1)} %xs_ref.1, bf16[2048,512]{1,0:T(8,128)(2,1)} %xs_ref.1, ...), custom_call_target="tpu_custom_call" | custom-call | tf_op jit(solution)/shard_map/back/pallas_call | solution.py:1654
  184.1 7.7 %finish.1 = (bf16[2048,512]{1,0:T(8,128)(2,1)}, f32[2048,512]{1,0:T(8,128)}, f32[64,512]{1,0:T(8,128)}, f32[64,512]{1,0:T(8,128)}, f32[64,512]{1,0:T(8,128)}, /*...) custom-call(bf16[2048,512]{1,0:T(8,128)(2,1)} %get-tuple-element.51., ...), custom_call_target="tpu_custom_call" | custom-call | tf_op jit(solution)/shard_map/finish/pallas_call | solution.py:1791

commit v3 on v2

--- a/solution.py
+++ b/solution.py
@@ -523,7 +523,7 @@
     do_ref[...] = dot_nt(branch, w_out()).astype(BF16)
 
 
-def pack_grads(count, part, gwo_ref, gwh_ref, gwr_ref, put):
+def pack_grads(count, part, gwo_ref, gwh_ref, gwr_ref, put, done=lambda first, slabs: None):
     half = count // 2
     for q in range(4):
         x, c = q // 2, q % 2
@@ -536,6 +536,7 @@
             put(1, over_y, slice(512, 640), out_part[:, y])
             for j in range(4):
                 put(1, over_y, slice(j * 128, (j + 1) * 128), turned[:, y, j])
+            done((over_x, over_y), half)
 
 
 def feed_kernel(
@@ -597,7 +598,7 @@
     for _ in range(5):
         groups_of_sems.append(bundle(sems[:11]))
         sems = sems[11:]
-    small_send, small_recv, state_send, state_recv, out_sem, stage_sem, fed_sem = sems
+    small_send, small_recv, state_send, state_recv, out_sem, stage_sem, fed_sem, pack_sem = sems
     main = Gather(count, mine, w_all, D, 3 * D, False, groups_of_sems[0])
     q_piece = Gather(count, mine, w_all, 0, D, False, groups_of_sems[1])
     o_piece = Gather(count, mine_o, r.wo_all, 0, D, True, groups_of_sems[2])
@@ -837,13 +838,17 @@
                 values.reshape(n, -1).astype(BF16)
             )
 
-        pack_grads(count, part, r.gwo, r.gwh, r.gwr, put)
-        copies = [
-            pltpu.make_async_copy(qkvf.at[:, 0:D], r.pack, out_sem.at[0]),
-            pltpu.make_async_copy(qkvf.at[:, D:1152], r.pack_r, out_sem.at[1]),
-        ]
-        for copy in copies:
-            copy.start()
+        copies = []
+
+        def done(first, slabs):
+            for slab, lanes, out in zip(first, (slice(0, D), slice(D, 1152)), (r.pack, r.pack_r)):
+                here = pl.ds(slab * part, slabs * part)
+                copies.append(
+                    pltpu.make_async_copy(qkvf.at[here, lanes], out.at[here], pack_sem.at[len(copies)])
+                )
+                copies[-1].start()
+
+        pack_grads(count, part, r.gwo, r.gwh, r.gwr, put, done)
         last = x_ref.shape[0] // FEED_ROWS - 1
         for copy in (*fed_copies(last - 1), *fed_copies(last), *copies):
             copy.wait()
@@ -933,7 +938,8 @@
         scratch_shapes=list(scratch.values())
         + gather_sems(count, True)
         + gather_sems(count, False) * 4
-        + [dma((count,)), dma((count,)), dma((3, 2)), dma((3, 2)), dma((2,)), dma((2, 3)), dma((2, 3))],
+        + [dma((count,)), dma((count,)), dma((3, 2)), dma((3, 2)), dma((2,)), dma((2, 3)), dma((2, 3))]
+        + [dma((16,))],
         compiler_params=pltpu.CompilerParams(
             vmem_limit_bytes=62 * MIB, collective_id=1, has_side_effects=True
         ),
@@ -1547,6 +1553,15 @@
     def _(u):
         at_chunk = step * per + u
 
+        def events(first):
+            for when, actions in schedule.items():
+                if first <= when < first + 8:
+
+                    @pl.when(at_chunk == when)
+                    def _(actions=actions):
+                        for action in actions:
+                            action()
+
         @pl.when(at_chunk < QUERY)
         def _():
             n, here, block, col, row = chunk(u, 0)
@@ -1561,6 +1576,7 @@
                 col, row, edge_ref,
                 reading.at[here], numer.at[here], total.at[here], head, aside,
             )
+            events(0)
 
         @pl.when((at_chunk >= QUERY) & (at_chunk < COLUMN))
         def _():
@@ -1569,6 +1585,7 @@
                 n, qkvf_ref.at[block], kept_ref.at[pl.ds(u, 1)], col, row, edge_ref,
                 numer.at[here], d_all.at[here, 0:D],
             )
+            events(QUERY)
 
         @pl.when((at_chunk >= COLUMN) & (at_chunk < SLOT))
         def _():
@@ -1577,6 +1594,7 @@
                 n, qkvf_ref.at[block], do_ref.at[block], reading.at[here], numer.at[here],
                 total.at[here], col, row, edge_ref, state, snap, snap_rows, d_all.at[here],
             )
+            events(COLUMN)
 
         @pl.when((at_chunk >= SLOT) & (at_chunk < INPUT))
         def _():
@@ -1585,6 +1603,7 @@
                 n, qkvf_ref.at[block], do_ref.at[block], reading.at[here], numer.at[here],
                 total.at[here], col, row, edge_ref, snap, snap_rows, d_all.at[here],
             )
+            events(SLOT)
 
         @pl.when((at_chunk >= INPUT) & (u == 0))
         def _():
@@ -1607,12 +1626,9 @@
             gi_held[lax.rem(nth, 2)] = dy_ref[...] + norm_back(unit, scale, small_ref[0:1], grad)
             give(nth).start()
 
-        for when, actions in schedule.items():
-
-            @pl.when(at_chunk == when)
-            def _(actions=actions):
-                for action in actions:
-                    action()
+        @pl.when(at_chunk >= INPUT)
+        def _():
+            events(INPUT)
 
     @pl.when(step + 2 < QUERY // per)
     def _():

time: 192 us -> 189 us (0.984)
  Pallas kernels: 191 us -> 188 us
    pallas_call x1, Pallas kernels: 85.2 us -> 82.7 us  [back(): pl.pallas_call(functools.partial(back_kernel, count, per), grid=(5 * bloc...]
where the time goes in v3:
time: 189 us
  Pallas kernels  188 us (99%)
    pallas_call x1, Pallas kernels, front(): pl.pallas_call(functools.partial(front_kernel, count, joined, (*ins, *out...  97.6 us
    pallas_call x1, Pallas kernels, back(): pl.pallas_call(functools.partial(back_kernel, count, per), grid=(5 * bloc...  82.7 us
    pallas_call x1, Pallas kernels, finish(): pl.pallas_call(functools.partial(finish_kernel, count, part), in_specs=[a...  7.71 us

profile of v3, /device:TPU:0, one launch (start us, length us, event | category | flops | bytes accessed | tf_op | source)
XLA Modules:
  0.0 188.8 jit_solution(7368805048792955582)
XLA Ops:
  0.7 97.6 %front.1 = (bf16[2048,2048]{1,0:T(8,128)(2,1)}, f32[2048,512]{1,0:T(8,128)}, f32[2048,512]{1,0:T(8,128)}, f32[2048,512]{1,0:T(8,128)}, f32[8,128,512]{2,1,0:T(8,...) custom-call(bf16[2048,512]{1,0:T(8,128)(2,1)} %xs_ref.1, ...), custom_call_target="tpu_custom_call" | custom-call | tf_op jit(solution)/shard_map/front/pallas_call | solution.py:932
  98.3 82.7 %back.1 = (f32[2048,512]{1,0:T(8,128)}, f32[4,64,512]{2,1,0:T(8,128)}, f32[4,64,640]{2,1,0:T(8,128)}, f32[4,64,128]{2,1,0:T(8,128)}, f32[4,64,256]{2,1,0:T(8,128...) custom-call(bf16[2048,512]{1,0:T(8,128)(2,1)} %xs_ref.1, bf16[2048,512]{1,0:T(8,128)(2,1)} %xs_ref.1, ...), custom_call_target="tpu_custom_call" | custom-call | tf_op jit(solution)/shard_map/back/pallas_call | solution.py:1670
  180.9 7.7 %finish.1 = (bf16[2048,512]{1,0:T(8,128)(2,1)}, f32[2048,512]{1,0:T(8,128)}, f32[64,512]{1,0:T(8,128)}, f32[64,512]{1,0:T(8,128)}, f32[64,512]{1,0:T(8,128)}, /*...) custom-call(bf16[2048,512]{1,0:T(8,128)(2,1)} %get-tuple-element.51., ...), custom_call_target="tpu_custom_call" | custom-call | tf_op jit(solution)/shard_map/finish/pallas_call | solution.py:1807
